TPU v7x, 32 devices: a whole 2x2x4 slice. The times are simulated.
32 devices in a mesh: groups: 2 (over x), chan: 16 (over z, y, core).
Axes of the slice: x: 2, y: 2, z: 4, core: 2. Of those that a mesh axis runs over, the one named last changes fastest.
Arguments:
- raw: bfloat16 [5120, 4096], P('chan', 'groups'), parts along dimension 1, may hold values from -50 to 50
- taps: bfloat16 [255], replicated, may hold values from -0.375 to 0.375
- tile_dist: int32 [16, 8], P('chan', 'groups'), parts along dimension 1, may hold values from 1 to 4, as said below
- tile_count: int32 [32], P(('groups', 'chan')), parts along dimension 0, may hold values from 0 to 4
- owner: int32 [8], P('groups'), parts along dimension 0, may hold values from 0 to 15, as said below
Outputs:
- band_stack: float32 [16, 256, 128], P('chan', 'groups'), parts along dimension 1
There are 2 independent parts, one for each index of `groups`. A program takes and returns all parts, laid end to end along the dimension named above; an argument that names none is the same for every part. Nothing has to cross between parts.
Inputs may be any that keep to these rules, and one draw needn't show every extreme that they name: Each row of tile_dist holds every distance of 1 to 4 once; in row i the first tile_count[i] entries d satisfy i + d < 16. `owner`: the owners are distinct, and some band is owned by index 15.
All inputs are finite; a program needn't handle non-finite values.
Results may differ from a plain program's by a relative error of at most 0.014.
Values may be sent and summed in bfloat16 or wider, within the bound.
A program may use at most 128 MiB of HBM per device.

v0:
```python
import functools
import math

import jax
import jax.numpy as jnp
from jax import lax
from jax.experimental import pallas as pl
from jax.experimental.pallas import tpu as pltpu
from jax.sharding import PartitionSpec as P

MESH = pl.DeviceIdType.MESH


def extended(x, sides, width):
    for axis, dim in sides:
        size, length = (lax.axis_size(axis), x.shape[dim])
        up = [(i, (i + 1) % size) for i in range(size - 1)]
        down = [(j, i) for i, j in up]
        last = lax.slice_in_dim(x, length - width, length, axis=dim)
        initial = lax.slice_in_dim(x, 0, width, axis=dim)
        before = lax.ppermute(last, axis, up)
        after = lax.ppermute(initial, axis, down)
        x = jnp.concatenate([before, x, after], axis=dim)
    return x


def passed_along(x, axis, by):
    size = lax.axis_size(axis)
    pairs = [(i, i + by) for i in range(size) if 0 <= i + by < size]
    return lax.ppermute(x, axis, pairs)


def band_matrix(taps, out_rows, in_cols):
    period = in_cols + 5
    padded = jnp.pad(taps, (0, period - taps.shape[0]))
    return jnp.tile(padded, out_rows)[: out_rows * in_cols].reshape(out_rows, in_cols)


def whiten(block):
    length, channels = block.shape
    bins = length // 16
    freqs = jnp.arange(1, bins + 1, dtype=jnp.int32)[:, None]
    times = jnp.arange(length, dtype=jnp.int32)[None, :]
    angle = (freqs * times % length).astype(jnp.float32) * (2.0 * math.pi / length)
    table = jnp.concatenate([jnp.cos(angle), -jnp.sin(angle)], axis=0)
    table_high = table.astype(jnp.bfloat16)
    table_low = (table - table_high.astype(jnp.float32)).astype(jnp.bfloat16)
    spectrum = jnp.dot(table_high, block, preferred_element_type=jnp.float32)
    spectrum = spectrum + jnp.dot(table_low, block, preferred_element_type=jnp.float32)
    squares = spectrum * spectrum
    power = jnp.sum(squares[:bins] + squares[bins:], axis=1) / (2 * channels)
    gain = lax.rsqrt(power + 1e-06)
    return (spectrum * jnp.concatenate([gain, gain])[:, None]).astype(jnp.bfloat16)


def cross_tile(mine, partner, scale):
    product = lax.dot_general(
        mine, partner, (((0,), (0,)), ((), ())), preferred_element_type=jnp.float32
    )
    return product * scale


def streamed(raw, taps, tile_dist, tile_count, owner):
    rows = raw.shape[0]
    width = taps.shape[0]
    half = (width - 1) // 2
    out_rows = rows // 5
    banded = band_matrix(taps, out_rows, rows + 2 * half)
    padded = extended(raw, (("chan", 0),), half)
    filtered = jnp.dot(banded, padded, preferred_element_type=jnp.float32)
    decimated = filtered.astype(jnp.bfloat16)
    regrouped = lax.all_to_all(decimated, "chan", split_axis=1, concat_axis=0, tiled=True)
    whitened = whiten(regrouped)
    channels = whitened.shape[1]
    scale = 1.0 / whitened.shape[0]
    bands = tile_dist.shape[1]
    slots = jnp.arange(bands, dtype=jnp.int32) < tile_count[0]
    stacks = []
    for distance in range(1, bands + 1):
        partner = passed_along(whitened, "chan", -distance)
        listed = jnp.sum(((tile_dist[0] == distance) & slots).astype(jnp.int32))
        tile = lax.cond(
            listed > 0,
            lambda first, second: cross_tile(first, second, scale),
            lambda first, second: jnp.zeros((channels, channels), jnp.float32),
            whitened,
            partner,
        )
        stacks.append(tile)
    stacked = jnp.stack(stacks)
    totals = lax.psum(stacked, "chan")
    selected = (owner == lax.axis_index("chan")).astype(jnp.float32)
    return jnp.einsum("b,bxy->xy", selected, totals, precision=lax.Precision.HIGHEST)[None]


def split(x):
    high = x.astype(jnp.bfloat16)
    low = (x - high.astype(jnp.float32)).astype(jnp.bfloat16)
    return high, low


def mm(a, b):
    return jnp.dot(a, b, preferred_element_type=jnp.float32)


def fused_kernel(
    n, width, bands,
    plan_hbm, raw_hbm, taps_ref, out_ref,
    plan_ref, raw_ref, loads, both, pair, send1, recv1, both2, pair2, send2, recv2, send3, ss0, rs0, ss4, rs4, ss1, rs1, ss2, rs2, ss3, rs3,
):
    me = lax.axis_index("chan")
    chips = n // 2
    chip, core = me // 2, me % 2
    rows, channels = raw_ref.shape
    block = channels // n
    steps = rows // 5
    length = steps * n
    bins = length // 16
    mine = 2 * bins // n
    hc = channels // 2
    window = 128
    lead = (window - steps) // 2

    loaded = [
        pltpu.make_async_copy(source, held, loads.at[at])
        for at, (source, held) in enumerate(
            [
                (raw_hbm, raw_ref),
                (plan_hbm, plan_ref),
            ]
        )
    ]
    for load in loaded:
        load.start()
    barrier = pltpu.get_barrier_semaphore()
    for k in range(1, n):
        pl.semaphore_signal(
            barrier, inc=1, device_id={"chan": lax.rem(me + k, n)}, device_id_type=MESH
        )

    lanes = taps_ref.shape[1]
    taps = jnp.broadcast_to(taps_ref[...], (8, taps_ref.shape[1]))
    first = pltpu.roll(taps, 0, 1, stride=5, stride_axis=0)
    banded = jnp.concatenate(
        [pltpu.roll(first, 40 * q, 1)[:, :384] for q in range(window // 8)], axis=0
    ).astype(jnp.bfloat16)[:, :rows]
    row = lax.broadcasted_iota(jnp.int32, (2 * bins, window), 0)
    col = lax.broadcasted_iota(jnp.int32, (2 * bins, window), 1)
    place = row % mine
    order = row // mine
    holder = (order % chips) * 2 + order // chips
    freq = holder * (mine // 2) + place % (mine // 2) + 1
    time = me * steps - lead + col
    turn = (freq * time + jnp.where(place >= mine // 2, length // 4, 0)) & (length - 1)
    table = jnp.cos(turn.astype(jnp.float32) * (2.0 * math.pi / length))
    table = jnp.where((time >= 0) & (time < length), table, 0.0)
    table_high, table_low = split(table)
    gmap = mm(table_high, banded) + mm(table_low, banded)
    gmap_high, gmap_low = split(gmap)

    for load in loaded:
        load.wait()
    chunk = 256

    def transform(c):
        halves = []
        for h in range(2):
            part = raw_ref[:, h * hc + c * chunk : h * hc + (c + 1) * chunk]
            spectra = mm(gmap_high, part) + mm(gmap_low, part)
            halves.append(spectra.reshape(n, mine, chunk))
        both[:, :, c * chunk : (c + 1) * chunk] = jnp.concatenate(halves, axis=1).astype(
            jnp.bfloat16
        )

    pieces = [(0, hc // 2), (hc // 2, hc // 2 + 128)]
    for c in range(hc // chunk // 2):
        transform(c)
    line = lax.broadcasted_iota(jnp.int32, (2 * mine, 128), 0)
    info = jnp.zeros((2 * mine, 128), jnp.float32)
    for d in range(bands):
        listed = jnp.int32(0)
        for s in range(bands):
            hit = (plan_ref[s] == d + 1) & (s < plan_ref[2 * bands])
            listed = listed + hit.astype(jnp.int32)
        info = jnp.where(line == core * mine + d, listed.astype(jnp.float32), info)
    both[:, :, hc:] = jnp.broadcast_to(info[None], (n, 2 * mine, 128)).astype(jnp.bfloat16)

    pl.semaphore_wait(barrier, n - 1)

    def copy0(p):
        cols = pl.ds(*pieces[p])
        return pltpu.make_async_remote_copy(
            src_ref=both.at[pl.ds((1 - core) * chips, chips), :, cols],
            dst_ref=pair.at[:, :, cols], send_sem=ss0.at[p], recv_sem=rs0.at[p],
            device_id={"chan": chip * 2 + 1 - core}, device_id_type=MESH,
        )

    def copy1(p, k):
        to = lax.rem(chip + k, chips)
        cols = pl.ds(*pieces[p])
        return pltpu.make_async_remote_copy(
            src_ref=send1.at[to, :, cols], dst_ref=recv1.at[chip, :, cols],
            send_sem=ss1.at[p * chips + k], recv_sem=rs1.at[p * chips + k],
            device_id={"chan": to * 2 + core}, device_id_type=MESH,
        )

    second_copy = pltpu.make_async_remote_copy(
        src_ref=both2.at[pl.ds((1 - core) * chips, chips)], dst_ref=pair2, send_sem=ss4,
        recv_sem=rs4, device_id={"chan": chip * 2 + 1 - core}, device_id_type=MESH,
    )

    def copy2(k):
        to = lax.rem(chip + k, chips)
        return pltpu.make_async_remote_copy(
            src_ref=send2.at[to], dst_ref=recv2.at[chip], send_sem=ss2.at[k],
            recv_sem=rs2.at[k], device_id={"chan": to * 2 + core}, device_id_type=MESH,
        )

    share = block // n
    place = (core * chips + chip) * share

    def copy3(k):
        to = lax.rem(me + k, n)
        return pltpu.make_async_remote_copy(
            src_ref=send3.at[to], dst_ref=out_ref.at[0, pl.ds(place, share)],
            send_sem=ss3.at[k], recv_sem=rs3.at[k], device_id={"chan": to}, device_id_type=MESH,
        )

    copy0(0).start()
    for c in range(hc // chunk // 2, hc // chunk):
        transform(c)
    copy0(1).start()
    for p in range(2):
        cols = slice(pieces[p][0], sum(pieces[p]))
        copy0(p).wait_recv()
        for k in range(1, chips):
            to = lax.rem(chip + k, chips)
            own = both[core * chips + to, :, cols].astype(jnp.float32)
            send1[to, :, cols] = (own + pair[to, :, cols].astype(jnp.float32)).astype(jnp.bfloat16)
            copy1(p, k).start()
        own = both[core * chips + chip, :, cols].astype(jnp.float32)
        recv1[chip, :, cols] = (own + pair[chip, :, cols].astype(jnp.float32)).astype(jnp.bfloat16)
    for p in range(2):
        for k in range(1, chips):
            copy1(p, k).wait_recv()
    total = recv1[0, :, :hc].astype(jnp.float32)
    for i in range(1, chips):
        total = total + recv1[i, :, :hc].astype(jnp.float32)

    white = []
    for j in range(n):
        h, at = divmod(j * block, hc)
        part = total[h * mine : (h + 1) * mine, at : at + block]
        squares = part * part
        squares = squares + pltpu.roll(squares, mine // 2, 0)
        power = jnp.sum(squares, axis=1, keepdims=True) / (2 * block)
        white.append(part * lax.rsqrt(power + 1e-06))
    left = jnp.concatenate(white, axis=0).astype(jnp.bfloat16)
    weights = [recv1[i, :, hc:].astype(jnp.float32) for i in range(chips)]
    rights = []
    for d in range(bands):
        tiles = []
        for i in range(n):
            if i + d + 1 < n:
                tiles.append(white[i + d + 1] * weights[i // 2][i % 2 * mine + d : i % 2 * mine + d + 1, :])
            else:
                tiles.append(jnp.zeros((mine, block), jnp.float32))
        rights.append(jnp.concatenate(tiles, axis=0).astype(jnp.bfloat16))
    right = jnp.concatenate(rights, axis=1)
    stacks = lax.dot_general(
        left, right, (((0,), (0,)), ((), ())), preferred_element_type=jnp.float32
    )
    hb = bands // 2 * block
    stacks = jnp.concatenate(
        [stacks[:, :hb].reshape(n, share, hb), stacks[:, hb:].reshape(n, share, hb)], axis=1
    )
    both2[...] = stacks.astype(jnp.bfloat16)

    second_copy.start()
    second_copy.wait_recv()
    for k in range(1, chips):
        to = lax.rem(chip + k, chips)
        own = both2[core * chips + to].astype(jnp.float32)
        send2[to] = (own + pair2[to].astype(jnp.float32)).astype(jnp.bfloat16)
        copy2(k).start()
    own = both2[core * chips + chip].astype(jnp.float32)
    recv2[chip] = (own + pair2[chip].astype(jnp.float32)).astype(jnp.bfloat16)
    for k in range(1, chips):
        copy2(k).wait_recv()
    total = recv2[0].astype(jnp.float32)
    for i in range(1, chips):
        total = total + recv2[i].astype(jnp.float32)
    total = total * (1.0 / (2 * bins))

    for to in range(n):
        chosen = jnp.zeros((share, block), jnp.float32)
        for d in range(bands):
            h, at = divmod(d * block, hb)
            owned = (plan_ref[bands + d] == to).astype(jnp.float32)
            chosen = chosen + total[h * share : (h + 1) * share, at : at + block] * owned
        send3[to] = chosen
    for k in range(1, n):
        copy3(k).start()
    out_ref[0, pl.ds(place, share)] = send3[me]
    for k in range(1, n):
        copy3(k).wait_recv()
    for p in range(2):
        copy0(p).wait_send()
        for k in range(1, chips):
            copy1(p, k).wait_send()
    second_copy.wait_send()
    for k in range(1, chips):
        copy2(k).wait_send()
    for k in range(1, n):
        copy3(k).wait_send()


def fused(raw, taps, tile_dist, tile_count, owner):
    n = lax.axis_size("chan")
    rows, channels = raw.shape
    width = taps.shape[0]
    half = (width - 1) // 2
    bands = tile_dist.shape[1]
    block = channels // n
    steps = rows // 5
    mine = 2 * (steps * n // 16) // n
    lead = (128 - steps) // 2
    lanes = 1024
    start = lanes - 5 * lead - half
    line = jnp.pad(taps.astype(jnp.float32), (start, lanes - start - width))
    line = line[None]
    plan = jnp.concatenate([tile_dist[0], owner, tile_count])
    vmem, hbm = pl.BlockSpec(memory_space=pltpu.VMEM), pl.BlockSpec(memory_space=pltpu.HBM)
    share = block // n
    sems = [pltpu.SemaphoreType.DMA((n,)) for _ in range(6)]
    return pl.pallas_call(
        functools.partial(fused_kernel, n, width, bands),
        out_shape=jax.ShapeDtypeStruct((1, block, block), jnp.float32),
        in_specs=[hbm, hbm, vmem],
        out_specs=vmem,
        scratch_shapes=[
            pltpu.SMEM(plan.shape, jnp.int32),
            pltpu.VMEM(raw.shape, raw.dtype),
            pltpu.SemaphoreType.DMA((2,)),
            pltpu.VMEM((n, 2 * mine, channels // 2 + 128), jnp.bfloat16),
            pltpu.VMEM((n // 2, 2 * mine, channels // 2 + 128), jnp.bfloat16),
            pltpu.VMEM((n // 2, 2 * mine, channels // 2 + 128), jnp.bfloat16),
            pltpu.VMEM((n // 2, 2 * mine, channels // 2 + 128), jnp.bfloat16),
            pltpu.VMEM((n, 2 * share, bands // 2 * block), jnp.bfloat16),
            pltpu.VMEM((n // 2, 2 * share, bands // 2 * block), jnp.bfloat16),
            pltpu.VMEM((n // 2, 2 * share, bands // 2 * block), jnp.bfloat16),
            pltpu.VMEM((n // 2, 2 * share, bands // 2 * block), jnp.bfloat16),
            pltpu.VMEM((n, share, block), jnp.float32),
            pltpu.SemaphoreType.DMA((2,)),
            pltpu.SemaphoreType.DMA((2,)),
            pltpu.SemaphoreType.DMA,
            pltpu.SemaphoreType.DMA,
            *sems,
        ],
        compiler_params=pltpu.CompilerParams(
            collective_id=0, has_side_effects=True, vmem_limit_bytes=int(53.25 * 2**20)
        ),
    )(plan, raw, line)


def shards(raw, taps, tile_dist, tile_count, owner):
    n = lax.axis_size("chan")
    rows, channels = raw.shape
    steps = rows // 5
    fits = (
        channels == 128 * n
        and n == 16
        and rows == 320
        and taps.shape[0] == 255
        and tile_dist.shape[1] == 4
    )
    path = fused if fits else streamed
    return path(raw, taps, tile_dist, tile_count, owner)


def solution(mesh):
    in_specs = (P("chan", "groups"), P(), P("chan", "groups"), P(("groups", "chan")), P("groups"))
    out_specs = P("chan", "groups", None)
    return jax.shard_map(shards, mesh=mesh, in_specs=in_specs, out_specs=out_specs, check_vma=False)
```

profile of v0, /device:TPU:1, one launch (start us, length us, event | category | flops | bytes accessed | tf_op | source)
XLA Modules:
  0.0 27.6 jit_solution(655621986947479351)
XLA Ops:
  0.7 0.7 %pad_add_fusion.plan_hbm = s32[9]{0:T(128)S(1)} fusion(s32[1]{0:T(128)S(6)} %copy.7, s32[4]{0:T(128)} %param.9, s32[4]{0:T(128)} %bitcast.3), kind=kLoop, calls=%fused_computation.1 | loop fusion | flops 18 | bytes 72 | tf_op jit(solution)/shard_map/concatenate | solution.py:332
  1.4 0.7 %pad_convert_fusion = f32[1024]{0:T(1024)S(1)} fusion(bf16[255]{0:T(256)(128)(2,1)} %param.6), kind=kLoop, calls=%fused_computation | loop fusion | flops 1024 | bytes 4606 | tf_op jit(solution)/shard_map/broadcast_in_dim | solution.py:331
  2.1 24.9 %shard_map.55 = f32[1,128,128]{2,1,0:T(8,128)S(1)} custom-call(s32[9]{0:T(128)S(1)} %pad_add_fusion.plan_hbm, bf16[320,2048]{1,0:T(8,128)(2,1)} %raw_hbm.1, f32[1,1024]{1,0:T(1,128)S(1)} %bitcast.2), custom_call_target="tpu_custom_call" | custom-call | tf_op jit(solution)/shard_map/pallas_call | solution.py:336
  27.0 0.6 %copy.8 = f32[1,128,128]{2,1,0:T(8,128)} copy(f32[1,128,128]{2,1,0:T(8,128)S(1)} %shard_map.55) | data formatting | bytes 131072
where the time goes:
time: 28.2 us; the launch traced here: 27.6 us
  Pallas kernels  24.9 us (88%)
  other arithmetic  1.48 us (5%)
  between operations  0.66 us (2%)
  local copies, waits for them, and re-layouts  0.63 us (2%)
    pallas_call x1, Pallas kernels, fused(): pl.pallas_call(functools.partial(fused_kernel, n, width, bands), out_shap...  24.9 us
    concatenate x1, other arithmetic, fused(): plan = jnp.concatenate([tile_dist[0], owner, tile_count])  0.75 us
    broadcast_in_dim x1, other arithmetic, fused(): line = line[None]  0.73 us
    unnamed x1, local copies, waits for them, and re-layouts  0.63 us

commit v1 on v0

v1 whole, which is shorter than its diff:
```python
import functools
import math

import jax
import jax.numpy as jnp
from jax import lax
from jax.experimental import pallas as pl
from jax.experimental.pallas import tpu as pltpu
from jax.sharding import PartitionSpec as P

MESH = pl.DeviceIdType.MESH


def extended(x, sides, width):
    for axis, dim in sides:
        size, length = (lax.axis_size(axis), x.shape[dim])
        up = [(i, (i + 1) % size) for i in range(size - 1)]
        down = [(j, i) for i, j in up]
        last = lax.slice_in_dim(x, length - width, length, axis=dim)
        initial = lax.slice_in_dim(x, 0, width, axis=dim)
        before = lax.ppermute(last, axis, up)
        after = lax.ppermute(initial, axis, down)
        x = jnp.concatenate([before, x, after], axis=dim)
    return x


def passed_along(x, axis, by):
    size = lax.axis_size(axis)
    pairs = [(i, i + by) for i in range(size) if 0 <= i + by < size]
    return lax.ppermute(x, axis, pairs)


def band_matrix(taps, out_rows, in_cols):
    period = in_cols + 5
    padded = jnp.pad(taps, (0, period - taps.shape[0]))
    return jnp.tile(padded, out_rows)[: out_rows * in_cols].reshape(out_rows, in_cols)


def whiten(block):
    length, channels = block.shape
    bins = length // 16
    freqs = jnp.arange(1, bins + 1, dtype=jnp.int32)[:, None]
    times = jnp.arange(length, dtype=jnp.int32)[None, :]
    angle = (freqs * times % length).astype(jnp.float32) * (2.0 * math.pi / length)
    table = jnp.concatenate([jnp.cos(angle), -jnp.sin(angle)], axis=0)
    table_high = table.astype(jnp.bfloat16)
    table_low = (table - table_high.astype(jnp.float32)).astype(jnp.bfloat16)
    spectrum = jnp.dot(table_high, block, preferred_element_type=jnp.float32)
    spectrum = spectrum + jnp.dot(table_low, block, preferred_element_type=jnp.float32)
    squares = spectrum * spectrum
    power = jnp.sum(squares[:bins] + squares[bins:], axis=1) / (2 * channels)
    gain = lax.rsqrt(power + 1e-06)
    return (spectrum * jnp.concatenate([gain, gain])[:, None]).astype(jnp.bfloat16)


def cross_tile(mine, partner, scale):
    product = lax.dot_general(
        mine, partner, (((0,), (0,)), ((), ())), preferred_element_type=jnp.float32
    )
    return product * scale


def streamed(raw, taps, tile_dist, tile_count, owner):
    rows = raw.shape[0]
    width = taps.shape[0]
    half = (width - 1) // 2
    out_rows = rows // 5
    banded = band_matrix(taps, out_rows, rows + 2 * half)
    padded = extended(raw, (("chan", 0),), half)
    filtered = jnp.dot(banded, padded, preferred_element_type=jnp.float32)
    decimated = filtered.astype(jnp.bfloat16)
    regrouped = lax.all_to_all(decimated, "chan", split_axis=1, concat_axis=0, tiled=True)
    whitened = whiten(regrouped)
    channels = whitened.shape[1]
    scale = 1.0 / whitened.shape[0]
    bands = tile_dist.shape[1]
    slots = jnp.arange(bands, dtype=jnp.int32) < tile_count[0]
    stacks = []
    for distance in range(1, bands + 1):
        partner = passed_along(whitened, "chan", -distance)
        listed = jnp.sum(((tile_dist[0] == distance) & slots).astype(jnp.int32))
        tile = lax.cond(
            listed > 0,
            lambda first, second: cross_tile(first, second, scale),
            lambda first, second: jnp.zeros((channels, channels), jnp.float32),
            whitened,
            partner,
        )
        stacks.append(tile)
    stacked = jnp.stack(stacks)
    totals = lax.psum(stacked, "chan")
    selected = (owner == lax.axis_index("chan")).astype(jnp.float32)
    return jnp.einsum("b,bxy->xy", selected, totals, precision=lax.Precision.HIGHEST)[None]


def split(x):
    high = x.astype(jnp.bfloat16)
    low = (x - high.astype(jnp.float32)).astype(jnp.bfloat16)
    return high, low


def mm(a, b):
    return jnp.dot(a, b, preferred_element_type=jnp.float32)


def fused_kernel(
    n, bands, pieces,
    raw_hbm, taps_hbm, dist_hbm, count_hbm, owner_hbm, out_ref,
    raw_ref, taps_ref, dist_ref, count_ref, owner_ref, loads, smalls,
    both, pair, send1, recv1, gath, ss0, rs0, ss1, rs1, ss2, rs2, ss3, rs3, ss4, rs4,
):
    me = lax.axis_index("chan")
    chips = n // 2
    chip, core = me // 2, me % 2
    other = chip * 2 + 1 - core
    rows, channels = raw_ref.shape
    block = channels // n
    steps = rows // 5
    length = steps * n
    bins = length // 16
    mine = 2 * bins // n
    hc = channels // 2
    width = hc // pieces
    window = 128
    lead = (window - steps) // 2
    half = (taps_hbm.shape[0] - 1) // 2
    lanes = 1024
    start = lanes - 5 * lead - half

    small = [
        pltpu.make_async_copy(source, held, smalls.at[at])
        for at, (source, held) in enumerate(
            [
                (taps_hbm, taps_ref),
                (dist_hbm, dist_ref),
                (count_hbm, count_ref),
                (owner_hbm, owner_ref),
            ]
        )
    ]
    for load in small:
        load.start()

    def load(p, h):
        cols = pl.ds(h * hc + p * width, width)
        return pltpu.make_async_copy(
            raw_hbm.at[:, cols], raw_ref.at[:, cols], loads.at[2 * p + h]
        )

    for p in range(pieces):
        for h in range(2):
            load(p, h).start()

    z, y = chip // 2, chip % 2

    def peer(k):
        far = [z, z + 1 - 2 * (z % 2), lax.rem(z + 2, 4), 3 - z][k // 2]
        return far * 2 + (1 - y if k % 2 else y)

    order = list(range(chips - 1, 0, -1))
    barrier = pltpu.get_barrier_semaphore()
    for k in order:
        pl.semaphore_signal(
            barrier, inc=1, device_id={"chan": peer(k) * 2 + core}, device_id_type=MESH
        )
    pl.semaphore_signal(barrier, inc=1, device_id={"chan": other}, device_id_type=MESH)

    row = lax.broadcasted_iota(jnp.int32, (2 * bins, window), 0)
    col = lax.broadcasted_iota(jnp.int32, (2 * bins, window), 1)
    place = row % mine
    rank = row // mine
    holder = (rank % chips) * 2 + rank // chips
    freq = holder * (mine // 2) + place % (mine // 2) + 1
    time = me * steps - lead + col
    turn = (freq * time + jnp.where(place >= mine // 2, length // 4, 0)) & (length - 1)
    table = jnp.cos(turn.astype(jnp.float32) * (2.0 * math.pi / length))
    table = jnp.where((time >= 0) & (time < length), table, 0.0)
    table_high, table_low = split(table)

    for load_one in small:
        load_one.wait()
    tap = taps_ref[...].astype(jnp.float32).reshape(1, -1)
    line = jnp.concatenate(
        [
            jnp.zeros((1, start), jnp.float32),
            tap,
            jnp.zeros((1, lanes - start - tap.shape[1]), jnp.float32),
        ],
        axis=1,
    )
    first = pltpu.roll(jnp.broadcast_to(line, (8, lanes)), 0, 1, stride=5, stride_axis=0)
    banded = jnp.concatenate(
        [pltpu.roll(first, 40 * q, 1)[:, :384] for q in range(window // 8)], axis=0
    ).astype(jnp.bfloat16)[:, :rows]
    gmap = mm(table_high, banded) + mm(table_low, banded)
    gmap_high, gmap_low = split(gmap)

    lines = lax.broadcasted_iota(jnp.int32, (2 * mine, 128), 0)
    info = jnp.zeros((2 * mine, 128), jnp.float32)
    for d in range(bands):
        listed = jnp.int32(0)
        for s in range(bands):
            hit = (dist_ref[0, s] == d + 1) & (s < count_ref[0])
            listed = listed + hit.astype(jnp.int32)
        info = jnp.where(lines == core * mine + d, listed.astype(jnp.float32), info)
    both[:, :, hc:] = jnp.broadcast_to(info[None], (n, 2 * mine, 128)).astype(jnp.bfloat16)
    chosen = [(owner_ref[d] == me).astype(jnp.float32) for d in range(bands)]

    def transform(p):
        halves = []
        for h in range(2):
            load(p, h).wait()
            part = raw_ref[:, h * hc + p * width : h * hc + (p + 1) * width]
            spectra = mm(gmap_high, part) + mm(gmap_low, part)
            halves.append(spectra.reshape(n, mine, width))
        both[:, :, p * width : (p + 1) * width] = jnp.concatenate(halves, axis=1).astype(
            jnp.bfloat16
        )

    def span(p, extra=128):
        return p * width, width + (extra if p == pieces - 1 else 0)

    def copy0(p):
        cols = pl.ds(*span(p))
        return pltpu.make_async_remote_copy(
            src_ref=both.at[pl.ds((1 - core) * chips, chips), :, cols],
            dst_ref=pair.at[:, :, cols], send_sem=ss0.at[p], recv_sem=rs0.at[p],
            device_id={"chan": other}, device_id_type=MESH,
        )

    def copy1(p, k):
        cols = pl.ds(*span(p))
        return pltpu.make_async_remote_copy(
            src_ref=send1.at[peer(k), :, cols], dst_ref=recv1.at[chip, :, cols],
            send_sem=ss1.at[p * chips + k], recv_sem=rs1.at[p * chips + k],
            device_id={"chan": peer(k) * 2 + core}, device_id_type=MESH,
        )

    def copy2(p, k):
        cols = pl.ds(*span(p, 0))
        return pltpu.make_async_remote_copy(
            src_ref=gath.at[me, :, cols], dst_ref=gath.at[me, :, cols],
            send_sem=ss2.at[p * chips + k], recv_sem=rs2.at[p * chips + k],
            device_id={"chan": peer(k) * 2 + core}, device_id_type=MESH,
        )

    def copy3(p, k):
        cols = pl.ds(*span(p, 0))
        source = peer(k) * 2 + core
        return pltpu.make_async_remote_copy(
            src_ref=gath.at[source, :, cols], dst_ref=gath.at[source, :, cols],
            send_sem=ss3.at[p * chips + k], recv_sem=rs3.at[p * chips + k],
            device_id={"chan": other}, device_id_type=MESH,
        )

    def copy4(p):
        cols = pl.ds(*span(p, 0))
        return pltpu.make_async_remote_copy(
            src_ref=gath.at[me, :, cols], dst_ref=gath.at[me, :, cols],
            send_sem=ss4.at[p], recv_sem=rs4.at[p],
            device_id={"chan": other}, device_id_type=MESH,
        )

    for p in range(pieces):
        transform(p)
    pl.semaphore_wait(barrier, chips)
    for p in range(pieces):
        copy0(p).start()
    for p in range(pieces):
        at, size = span(p)
        cols = slice(at, at + size)
        copy0(p).wait_recv()
        for k in order:
            to = peer(k)
            own = both[core * chips + to, :, cols].astype(jnp.float32)
            send1[to, :, cols] = (own + pair[to, :, cols].astype(jnp.float32)).astype(jnp.bfloat16)
            copy1(p, k).start()
        own = both[core * chips + chip, :, cols].astype(jnp.float32)
        recv1[chip, :, cols] = (own + pair[chip, :, cols].astype(jnp.float32)).astype(jnp.bfloat16)

    for p in range(pieces):
        for k in order:
            copy1(p, k).wait_recv()
        cols = slice(p * width, (p + 1) * width)
        total = recv1[0, :, cols].astype(jnp.float32)
        for i in range(1, chips):
            total = total + recv1[i, :, cols].astype(jnp.float32)
        squares = total * total
        white = []
        for b in range(width // block):
            at = slice(b * block, (b + 1) * block)
            power = jnp.sum(squares[:, at], axis=1, keepdims=True)
            turned = [
                pltpu.roll(power[h * mine : (h + 1) * mine], mine // 2, 0) for h in range(2)
            ]
            power = (power + jnp.concatenate(turned, axis=0)) / (2 * block)
            white.append(total[:, at] * lax.rsqrt(power + 1e-06))
        gath[me, :, cols] = jnp.concatenate(white, axis=1).astype(jnp.bfloat16)
        for k in order:
            copy2(p, k).start()
        copy4(p).start()

    weights = []
    for i in range(n):
        weight = jnp.zeros((1, 128), jnp.float32)
        for d in range(bands):
            at = i % 2 * mine + d
            weight = weight + recv1[i // 2, at : at + 1, hc:].astype(jnp.float32) * chosen[d]
        weights.append(jnp.broadcast_to(weight, (mine, block)))
    scales = [
        jnp.concatenate([weights[t], weights[t + n // 2]], axis=0) for t in range(n // 2)
    ]

    def products(source):
        held = gath[source].astype(jnp.float32)
        tiles = [held[:, t * block : (t + 1) * block] for t in range(n // 2)]
        left = [tiles[t] * scales[t] for t in range(n // 2)]
        for d in range(bands):
            tiles.append(
                jnp.concatenate([tiles[d][mine:], jnp.zeros((mine, block), jnp.float32)], axis=0)
            )
        right = []
        for t in range(n // 2):
            tile = tiles[t + 1] * chosen[0]
            for d in range(1, bands):
                tile = tile + tiles[t + d + 1] * chosen[d]
            right.append(tile)
        return left, right

    def add(total, at):
        left0, right0 = products(at * 2)
        left1, right1 = products(at * 2 + 1)
        left = jnp.concatenate(left0 + left1, axis=0).astype(jnp.bfloat16)
        right = jnp.concatenate(right0 + right1, axis=0).astype(jnp.bfloat16)
        return total + lax.dot_general(
            left, right, (((0,), (0,)), ((), ())), preferred_element_type=jnp.float32
        )

    near = order[::-1]
    for p in range(pieces):
        copy4(p).wait_recv()
        for k in near:
            copy2(p, k).wait_recv()
            copy3(p, k).start()
    result = add(jnp.zeros((block, block), jnp.float32), chip)
    for k in near:
        for p in range(pieces):
            copy3(p, k).wait_recv()
        result = add(result, peer(k))
    out_ref[0] = result * (1.0 / (2 * bins))

    for p in range(pieces):
        copy0(p).wait_send()
        copy4(p).wait_send()
        for k in order:
            copy1(p, k).wait_send()
            copy2(p, k).wait_send()
            copy3(p, k).wait_send()


def fused(raw, taps, tile_dist, tile_count, owner):
    n = lax.axis_size("chan")
    rows, channels = raw.shape
    bands = tile_dist.shape[1]
    block = channels // n
    steps = rows // 5
    mine = 2 * (steps * n // 16) // n
    chips = n // 2
    hc = channels // 2
    pieces = 4
    vmem, hbm = pl.BlockSpec(memory_space=pltpu.VMEM), pl.BlockSpec(memory_space=pltpu.HBM)
    dma = pltpu.SemaphoreType.DMA
    return pl.pallas_call(
        functools.partial(fused_kernel, n, bands, pieces),
        out_shape=jax.ShapeDtypeStruct((1, block, block), jnp.float32),
        in_specs=[hbm] * 5,
        out_specs=vmem,
        scratch_shapes=[
            pltpu.VMEM(raw.shape, raw.dtype),
            pltpu.VMEM(taps.shape, taps.dtype),
            pltpu.SMEM(tile_dist.shape, jnp.int32),
            pltpu.SMEM(tile_count.shape, jnp.int32),
            pltpu.SMEM(owner.shape, jnp.int32),
            dma((2 * pieces,)),
            dma((4,)),
            pltpu.VMEM((n, 2 * mine, hc + 128), jnp.bfloat16),
            pltpu.VMEM((chips, 2 * mine, hc + 128), jnp.bfloat16),
            pltpu.VMEM((chips, 2 * mine, hc + 128), jnp.bfloat16),
            pltpu.VMEM((chips, 2 * mine, hc + 128), jnp.bfloat16),
            pltpu.VMEM((n, 2 * mine, hc), jnp.bfloat16),
            dma((pieces,)),
            dma((pieces,)),
            dma((pieces * chips,)),
            dma((pieces * chips,)),
            dma((pieces * chips,)),
            dma((pieces * chips,)),
            dma((pieces * chips,)),
            dma((pieces * chips,)),
            dma((pieces,)),
            dma((pieces,)),
        ],
        compiler_params=pltpu.CompilerParams(
            collective_id=0, has_side_effects=True, vmem_limit_bytes=int(53.25 * 2**20)
        ),
    )(raw, taps, tile_dist, tile_count, owner)


def shards(raw, taps, tile_dist, tile_count, owner):
    n = lax.axis_size("chan")
    rows, channels = raw.shape
    steps = rows // 5
    fits = (
        channels == 128 * n
        and n == 16
        and rows == 320
        and taps.shape[0] == 255
        and tile_dist.shape[1] == 4
    )
    path = fused if fits else streamed
    return path(raw, taps, tile_dist, tile_count, owner)


def solution(mesh):
    in_specs = (P("chan", "groups"), P(), P("chan", "groups"), P(("groups", "chan")), P("groups"))
    out_specs = P("chan", "groups", None)
    return jax.shard_map(shards, mesh=mesh, in_specs=in_specs, out_specs=out_specs, check_vma=False)
```

time: 28.2 us -> 29.3 us (1.039)
  local copies, waits for them, and re-layouts: 0.63 us -> 2.59 us
  other arithmetic: 1.48 us -> 0 us
  Pallas kernels: 24.9 us -> 25.6 us
    unnamed x1 -> x7, local copies, waits for them, and re-layouts: 0.63 us -> 2.59 us
    pallas_call x1, Pallas kernels: 24.9 us -> 25.6 us  [fused(): pl.pallas_call(functools.partial(fused_kernel, n, bands, pieces), out_sha...]
    concatenate x1 -> x0, other arithmetic: 0.75 us -> none  [fused(): plan = jnp.concatenate([tile_dist[0], owner, tile_count])]
    broadcast_in_dim x1 -> x0, other arithmetic: 0.73 us -> none  [fused(): line = line[None]]
where the time goes in v1:
time: 29.3 us; the launch traced here: 28.9 us
  Pallas kernels  25.6 us (87%)
  local copies, waits for them, and re-layouts  2.59 us (9%)
  between operations  0.67 us (2%)
    pallas_call x1, Pallas kernels, fused(): pl.pallas_call(functools.partial(fused_kernel, n, bands, pieces), out_sha...  25.6 us
    unnamed x7, local copies, waits for them, and re-layouts  2.59 us

profile of v1, /device:TPU:1, one launch (start us, length us, event | category | flops | bytes accessed | tf_op | source)
XLA Modules:
  0.0 28.9 jit_solution(10993354667157222200)
XLA Ops:
  0.7 0.0 copy-start
  0.7 0.6 %copy-done = bf16[255]{0:T(256)(128)(2,1)S(1)} copy-done((bf16[255]{0:T(256)(128)(2,1)S(1)}, bf16[255]{0:T(256)(128)(2,1)}, u32[]{:S(2)}) %copy-start) | copy-done | bytes 534
  1.3 0.0 copy-start.1
  1.3 0.7 %copy-done.1 = s32[1,4]{1,0:T(1,128)S(1)} copy-done((s32[1,4]{1,0:T(1,128)S(1)}, s32[1,4]{1,0:T(1,128)}, u32[]{:S(2)}) %copy-start.1) | copy-done | bytes 40
  2.0 0.0 copy-start.2
  2.0 0.7 %copy-done.2 = s32[4]{0:T(128)S(1)} copy-done((s32[4]{0:T(128)S(1)}, s32[4]{0:T(128)}, u32[]{:S(2)}) %copy-start.2) | copy-done | bytes 40
  2.6 25.6 %shard_map.55 = f32[1,128,128]{2,1,0:T(8,128)S(1)} custom-call(bf16[320,2048]{1,0:T(8,128)(2,1)} %raw_hbm.1, bf16[255]{0:T(256)(128)(2,1)S(1)} %copy-done, s32[1,4]{1,0:T(1,128)S(1)} %copy-done.1, s32[1]{0:T(128)S(6)} %copy.7.count_hbm, s32[4]{0:T(128)S(1)} %copy-done.2), custom_call_target="tpu_custom_call" | custom-call | tf_op jit(solution)/shard_map/pallas_call | solution.py:373
  28.3 0.6 %copy.8 = f32[1,128,128]{2,1,0:T(8,128)} copy(f32[1,128,128]{2,1,0:T(8,128)S(1)} %shard_map.55) | data formatting | bytes 131072
Async XLA Ops:
  0.7 0.7 %copy-start = (bf16[255]{0:T(256)(128)(2,1)S(1)}, bf16[255]{0:T(256)(128)(2,1)}, u32[]{:S(2)}) copy-start(bf16[255]{0:T(256)(128)(2,1)} %taps_hbm.1) | copy-start | bytes 1534
  1.3 0.7 %copy-start.1 = (s32[1,4]{1,0:T(1,128)S(1)}, s32[1,4]{1,0:T(1,128)}, u32[]{:S(2)}) copy-start(s32[1,4]{1,0:T(1,128)} %dist_hbm.1) | copy-start | bytes 52
  2.0 0.7 %copy-start.2 = (s32[4]{0:T(128)S(1)}, s32[4]{0:T(128)}, u32[]{:S(2)}) copy-start(s32[4]{0:T(128)} %owner_hbm.1) | copy-start | bytes 52

commit v2 on v1

--- a/solution.py
+++ b/solution.py
@@ -107,7 +107,7 @@
     n, bands, pieces,
     raw_hbm, taps_hbm, dist_hbm, count_hbm, owner_hbm, out_ref,
     raw_ref, taps_ref, dist_ref, count_ref, owner_ref, loads, smalls,
-    both, pair, send1, recv1, gath, ss0, rs0, ss1, rs1, ss2, rs2, ss3, rs3, ss4, rs4,
+    both, pair, send1, recv1, same, cross, sent, rs0, rs1, rs2, rs3,
 ):
     me = lax.axis_index("chan")
     chips = n // 2
@@ -193,7 +193,7 @@
         [pltpu.roll(first, 40 * q, 1)[:, :384] for q in range(window // 8)], axis=0
     ).astype(jnp.bfloat16)[:, :rows]
     gmap = mm(table_high, banded) + mm(table_low, banded)
-    gmap_high, gmap_low = split(gmap)
+    gmap = gmap.astype(jnp.bfloat16)
 
     lines = lax.broadcasted_iota(jnp.int32, (2 * mine, 128), 0)
     info = jnp.zeros((2 * mine, 128), jnp.float32)
@@ -211,8 +211,7 @@
         for h in range(2):
             load(p, h).wait()
             part = raw_ref[:, h * hc + p * width : h * hc + (p + 1) * width]
-            spectra = mm(gmap_high, part) + mm(gmap_low, part)
-            halves.append(spectra.reshape(n, mine, width))
+            halves.append(mm(gmap, part).reshape(n, mine, width))
         both[:, :, p * width : (p + 1) * width] = jnp.concatenate(halves, axis=1).astype(
             jnp.bfloat16
         )
@@ -220,46 +219,44 @@
     def span(p, extra=128):
         return p * width, width + (extra if p == pieces - 1 else 0)
 
+    def remote(source, target, phase, sem, to):
+        return pltpu.make_async_remote_copy(
+            src_ref=source, dst_ref=target, send_sem=sent.at[phase], recv_sem=sem,
+            device_id={"chan": to}, device_id_type=MESH,
+        )
+
     def copy0(p):
         cols = pl.ds(*span(p))
-        return pltpu.make_async_remote_copy(
-            src_ref=both.at[pl.ds((1 - core) * chips, chips), :, cols],
-            dst_ref=pair.at[:, :, cols], send_sem=ss0.at[p], recv_sem=rs0.at[p],
-            device_id={"chan": other}, device_id_type=MESH,
+        return remote(
+            both.at[pl.ds((1 - core) * chips, chips), :, cols], pair.at[:, :, cols],
+            0, rs0.at[p], other,
         )
 
     def copy1(p, k):
         cols = pl.ds(*span(p))
-        return pltpu.make_async_remote_copy(
-            src_ref=send1.at[peer(k), :, cols], dst_ref=recv1.at[chip, :, cols],
-            send_sem=ss1.at[p * chips + k], recv_sem=rs1.at[p * chips + k],
-            device_id={"chan": peer(k) * 2 + core}, device_id_type=MESH,
+        return remote(
+            send1.at[k, :, cols], recv1.at[k, :, cols], 1, rs1.at[p], peer(k) * 2 + core
         )
 
     def copy2(p, k):
         cols = pl.ds(*span(p, 0))
-        return pltpu.make_async_remote_copy(
-            src_ref=gath.at[me, :, cols], dst_ref=gath.at[me, :, cols],
-            send_sem=ss2.at[p * chips + k], recv_sem=rs2.at[p * chips + k],
-            device_id={"chan": peer(k) * 2 + core}, device_id_type=MESH,
-        )
-
-    def copy3(p, k):
+        return remote(
+            same.at[0, :, cols], same.at[k, :, cols], 2, rs2.at[p], peer(k) * 2 + core
+        )
+
+    def copy3(p):
         cols = pl.ds(*span(p, 0))
-        source = peer(k) * 2 + core
-        return pltpu.make_async_remote_copy(
-            src_ref=gath.at[source, :, cols], dst_ref=gath.at[source, :, cols],
-            send_sem=ss3.at[p * chips + k], recv_sem=rs3.at[p * chips + k],
-            device_id={"chan": other}, device_id_type=MESH,
-        )
-
-    def copy4(p):
-        cols = pl.ds(*span(p, 0))
-        return pltpu.make_async_remote_copy(
-            src_ref=gath.at[me, :, cols], dst_ref=gath.at[me, :, cols],
-            send_sem=ss4.at[p], recv_sem=rs4.at[p],
-            device_id={"chan": other}, device_id_type=MESH,
-        )
+        return remote(same.at[:, :, cols], cross.at[:, :, cols], 3, rs3.at[p], other)
+
+    others = pl.ds(1, chips - 1)
+
+    def arrived1(p):
+        region = recv1.at[others, :, pl.ds(*span(p))]
+        remote(region, region, 1, rs1.at[p], other).wait_recv()
+
+    def arrived2(p):
+        region = same.at[others, :, pl.ds(*span(p, 0))]
+        remote(region, region, 2, rs2.at[p], other).wait_recv()
 
     for p in range(pieces):
         transform(p)
@@ -271,20 +268,20 @@
         cols = slice(at, at + size)
         copy0(p).wait_recv()
         for k in order:
-            to = peer(k)
-            own = both[core * chips + to, :, cols].astype(jnp.float32)
-            send1[to, :, cols] = (own + pair[to, :, cols].astype(jnp.float32)).astype(jnp.bfloat16)
+            own = both[core * chips + peer(k), :, cols].astype(jnp.float32)
+            send1[k, :, cols] = (own + pair[peer(k), :, cols].astype(jnp.float32)).astype(
+                jnp.bfloat16
+            )
             copy1(p, k).start()
         own = both[core * chips + chip, :, cols].astype(jnp.float32)
-        recv1[chip, :, cols] = (own + pair[chip, :, cols].astype(jnp.float32)).astype(jnp.bfloat16)
-
-    for p in range(pieces):
-        for k in order:
-            copy1(p, k).wait_recv()
+        recv1[0, :, cols] = (own + pair[chip, :, cols].astype(jnp.float32)).astype(jnp.bfloat16)
+
+    for p in range(pieces):
+        arrived1(p)
         cols = slice(p * width, (p + 1) * width)
         total = recv1[0, :, cols].astype(jnp.float32)
-        for i in range(1, chips):
-            total = total + recv1[i, :, cols].astype(jnp.float32)
+        for k in range(1, chips):
+            total = total + recv1[k, :, cols].astype(jnp.float32)
         squares = total * total
         white = []
         for b in range(width // block):
@@ -295,24 +292,23 @@
             ]
             power = (power + jnp.concatenate(turned, axis=0)) / (2 * block)
             white.append(total[:, at] * lax.rsqrt(power + 1e-06))
-        gath[me, :, cols] = jnp.concatenate(white, axis=1).astype(jnp.bfloat16)
+        same[0, :, cols] = jnp.concatenate(white, axis=1).astype(jnp.bfloat16)
         for k in order:
             copy2(p, k).start()
-        copy4(p).start()
 
     weights = []
     for i in range(n):
         weight = jnp.zeros((1, 128), jnp.float32)
         for d in range(bands):
             at = i % 2 * mine + d
-            weight = weight + recv1[i // 2, at : at + 1, hc:].astype(jnp.float32) * chosen[d]
+            weight = weight + recv1[peer(i // 2), at : at + 1, hc:].astype(jnp.float32) * chosen[d]
         weights.append(jnp.broadcast_to(weight, (mine, block)))
     scales = [
         jnp.concatenate([weights[t], weights[t + n // 2]], axis=0) for t in range(n // 2)
     ]
 
-    def products(source):
-        held = gath[source].astype(jnp.float32)
+    def products(held):
+        held = held.astype(jnp.float32)
         tiles = [held[:, t * block : (t + 1) * block] for t in range(n // 2)]
         left = [tiles[t] * scales[t] for t in range(n // 2)]
         for d in range(bands):
@@ -327,35 +323,34 @@
             right.append(tile)
         return left, right
 
-    def add(total, at):
-        left0, right0 = products(at * 2)
-        left1, right1 = products(at * 2 + 1)
-        left = jnp.concatenate(left0 + left1, axis=0).astype(jnp.bfloat16)
-        right = jnp.concatenate(right0 + right1, axis=0).astype(jnp.bfloat16)
+    def add(total, refs):
+        lefts, rights = [], []
+        for held in refs:
+            left, right = products(held)
+            lefts += left
+            rights += right
+        left = jnp.concatenate(lefts, axis=0).astype(jnp.bfloat16)
+        right = jnp.concatenate(rights, axis=0).astype(jnp.bfloat16)
         return total + lax.dot_general(
             left, right, (((0,), (0,)), ((), ())), preferred_element_type=jnp.float32
         )
 
-    near = order[::-1]
-    for p in range(pieces):
-        copy4(p).wait_recv()
-        for k in near:
-            copy2(p, k).wait_recv()
-            copy3(p, k).start()
-    result = add(jnp.zeros((block, block), jnp.float32), chip)
-    for k in near:
-        for p in range(pieces):
-            copy3(p, k).wait_recv()
-        result = add(result, peer(k))
+    for p in range(pieces):
+        arrived2(p)
+        copy3(p).start()
+    result = jnp.zeros((block, block), jnp.float32)
+    for k in range(0, chips, 2):
+        result = add(result, [same[k], same[k + 1]])
+    for p in range(pieces):
+        copy3(p).wait_recv()
+    for k in range(0, chips, 2):
+        result = add(result, [cross[k], cross[k + 1]])
     out_ref[0] = result * (1.0 / (2 * bins))
 
-    for p in range(pieces):
-        copy0(p).wait_send()
-        copy4(p).wait_send()
-        for k in order:
-            copy1(p, k).wait_send()
-            copy2(p, k).wait_send()
-            copy3(p, k).wait_send()
+    remote(pair, pair, 0, rs0.at[0], other).wait_send()
+    remote(recv1.at[others], recv1.at[others], 1, rs0.at[0], other).wait_send()
+    remote(same.at[others], same.at[others], 2, rs0.at[0], other).wait_send()
+    remote(same, same, 3, rs0.at[0], other).wait_send()
 
 
 def fused(raw, taps, tile_dist, tile_count, owner):
@@ -370,6 +365,7 @@
     pieces = 4
     vmem, hbm = pl.BlockSpec(memory_space=pltpu.VMEM), pl.BlockSpec(memory_space=pltpu.HBM)
     dma = pltpu.SemaphoreType.DMA
+    held = functools.partial(pltpu.with_memory_space_constraint, memory_space=pltpu.HBM)
     return pl.pallas_call(
         functools.partial(fused_kernel, n, bands, pieces),
         out_shape=jax.ShapeDtypeStruct((1, block, block), jnp.float32),
@@ -387,22 +383,18 @@
             pltpu.VMEM((chips, 2 * mine, hc + 128), jnp.bfloat16),
             pltpu.VMEM((chips, 2 * mine, hc + 128), jnp.bfloat16),
             pltpu.VMEM((chips, 2 * mine, hc + 128), jnp.bfloat16),
-            pltpu.VMEM((n, 2 * mine, hc), jnp.bfloat16),
+            pltpu.VMEM((chips, 2 * mine, hc), jnp.bfloat16),
+            pltpu.VMEM((chips, 2 * mine, hc), jnp.bfloat16),
+            dma((4,)),
             dma((pieces,)),
             dma((pieces,)),
-            dma((pieces * chips,)),
-            dma((pieces * chips,)),
-            dma((pieces * chips,)),
-            dma((pieces * chips,)),
-            dma((pieces * chips,)),
-            dma((pieces * chips,)),
             dma((pieces,)),
             dma((pieces,)),
         ],
         compiler_params=pltpu.CompilerParams(
             collective_id=0, has_side_effects=True, vmem_limit_bytes=int(53.25 * 2**20)
         ),
-    )(raw, taps, tile_dist, tile_count, owner)
+    )(held(raw), held(taps), held(tile_dist), tile_count, held(owner))
 
 
 def shards(raw, taps, tile_dist, tile_count, owner):

time: 29.3 us -> 25 us (0.85)
  Pallas kernels: 25.6 us -> 23.5 us
  local copies, waits for them, and re-layouts: 2.59 us -> 0.63 us
    pallas_call x1, Pallas kernels: 25.6 us -> 23.5 us  [fused(): pl.pallas_call(functools.partial(fused_kernel, n, bands, pieces), out_sha...]
    unnamed x7 -> x1, local copies, waits for them, and re-layouts: 2.59 us -> 0.63 us
where the time goes in v2:
time: 25 us; the launch traced here: 24.8 us
  Pallas kernels  23.5 us (94%)
  between operations  0.66 us (3%)
  local copies, waits for them, and re-layouts  0.63 us (3%)
    pallas_call x1, Pallas kernels, fused(): pl.pallas_call(functools.partial(fused_kernel, n, bands, pieces), out_sha...  23.5 us
    unnamed x1, local copies, waits for them, and re-layouts  0.63 us

profile of v2, /device:TPU:1, one launch (start us, length us, event | category | flops | bytes accessed | tf_op | source)
XLA Modules:
  0.0 24.8 jit_solution(14788698248363410308)
XLA Ops:
  0.7 23.5 %shard_map.55 = f32[1,128,128]{2,1,0:T(8,128)S(1)} custom-call(bf16[320,2048]{1,0:T(8,128)(2,1)} %raw_hbm.1, bf16[255]{0:T(256)(128)(2,1)} %taps_hbm.1, s32[1,4]{1,0:T(1,128)} %dist_hbm.1, s32[1]{0:T(128)S(6)} %copy.7.count_hbm, s32[4]{0:T(128)} %owner_hbm.1), custom_call_target="tpu_custom_call" | custom-call | tf_op jit(solution)/shard_map/pallas_call | solution.py:369
  24.2 0.6 %copy.8 = f32[1,128,128]{2,1,0:T(8,128)} copy(f32[1,128,128]{2,1,0:T(8,128)S(1)} %shard_map.55) | data formatting | bytes 131072

commit v3 on v2

--- a/solution.py
+++ b/solution.py
@@ -104,10 +104,10 @@
 
 
 def fused_kernel(
-    n, bands, pieces,
+    n, bands, widths, cuts,
     raw_hbm, taps_hbm, dist_hbm, count_hbm, owner_hbm, out_ref,
     raw_ref, taps_ref, dist_ref, count_ref, owner_ref, loads, smalls,
-    both, pair, send1, recv1, same, cross, sent, rs0, rs1, rs2, rs3,
+    both, pair, send1, recv1, same, cross, ready, info, info_cross, sent, rs0, rs1, rs2, rs3, rs4,
 ):
     me = lax.axis_index("chan")
     chips = n // 2
@@ -120,12 +120,55 @@
     bins = length // 16
     mine = 2 * bins // n
     hc = channels // 2
-    width = hc // pieces
+    pieces = len(widths)
+    starts = [sum(widths[:p]) for p in range(pieces)]
+    edges = [sum(cuts[:c]) for c in range(len(cuts))]
     window = 128
     lead = (window - steps) // 2
     half = (taps_hbm.shape[0] - 1) // 2
     lanes = 1024
     start = lanes - 5 * lead - half
+
+    z, y = chip // 2, chip % 2
+
+    def peer(k):
+        far = [z, z + 1 - 2 * (z % 2), lax.rem(z + 2, 4), 3 - z][k // 2]
+        return far * 2 + (1 - y if k % 2 else y)
+
+    order = list(range(chips - 1, 0, -1))
+
+    def slot(to):
+        low = y + to % 2 - 2 * y * (to % 2)
+        mid = z % 2 + to // 2 % 2 - 2 * (z % 2) * (to // 2 % 2)
+        high = z // 2 + to // 4 - 2 * (z // 2) * (to // 4)
+        return 4 * high + 2 * mid + low
+
+    def ranked(way):
+        if way == "rot":
+            tos = [lax.rem(chip + k, chips) for k in range(1, chips)]
+        elif way == "back":
+            tos = [lax.rem(chip + k, chips) for k in range(chips - 1, 0, -1)]
+        elif way == "xor":
+            return [(peer(k), k) for k in order]
+        else:
+            tos = [k + (k >= chip).astype(jnp.int32) for k in range(chips - 1)]
+            if way == "down":
+                tos = tos[::-1]
+        return [(to, slot(to)) for to in tos]
+
+    first_order = ranked("xor")
+    second_order = ranked("up")
+    barrier = pltpu.get_barrier_semaphore()
+
+    def greet(semaphore, to):
+        pl.semaphore_signal(semaphore, inc=1, device_id={"chan": to}, device_id_type=MESH)
+
+    @pl.when(core == 1)
+    def _():
+        greet(barrier, other)
+
+    for k in order:
+        greet(barrier, peer(k) * 2 + 1)
 
     small = [
         pltpu.make_async_copy(source, held, smalls.at[at])
@@ -142,28 +185,14 @@
         load.start()
 
     def load(p, h):
-        cols = pl.ds(h * hc + p * width, width)
+        cols = pl.ds(h * hc + edges[p], cuts[p])
         return pltpu.make_async_copy(
             raw_hbm.at[:, cols], raw_ref.at[:, cols], loads.at[2 * p + h]
         )
 
-    for p in range(pieces):
+    for c in range(len(cuts)):
         for h in range(2):
-            load(p, h).start()
-
-    z, y = chip // 2, chip % 2
-
-    def peer(k):
-        far = [z, z + 1 - 2 * (z % 2), lax.rem(z + 2, 4), 3 - z][k // 2]
-        return far * 2 + (1 - y if k % 2 else y)
-
-    order = list(range(chips - 1, 0, -1))
-    barrier = pltpu.get_barrier_semaphore()
-    for k in order:
-        pl.semaphore_signal(
-            barrier, inc=1, device_id={"chan": peer(k) * 2 + core}, device_id_type=MESH
-        )
-    pl.semaphore_signal(barrier, inc=1, device_id={"chan": other}, device_id_type=MESH)
+            load(c, h).start()
 
     row = lax.broadcasted_iota(jnp.int32, (2 * bins, window), 0)
     col = lax.broadcasted_iota(jnp.int32, (2 * bins, window), 1)
@@ -195,29 +224,29 @@
     gmap = mm(table_high, banded) + mm(table_low, banded)
     gmap = gmap.astype(jnp.bfloat16)
 
-    lines = lax.broadcasted_iota(jnp.int32, (2 * mine, 128), 0)
-    info = jnp.zeros((2 * mine, 128), jnp.float32)
+    lane = lax.broadcasted_iota(jnp.int32, (1, 128), 1)
+    row = jnp.zeros((1, 128), jnp.float32)
     for d in range(bands):
         listed = jnp.int32(0)
         for s in range(bands):
             hit = (dist_ref[0, s] == d + 1) & (s < count_ref[0])
             listed = listed + hit.astype(jnp.int32)
-        info = jnp.where(lines == core * mine + d, listed.astype(jnp.float32), info)
-    both[:, :, hc:] = jnp.broadcast_to(info[None], (n, 2 * mine, 128)).astype(jnp.bfloat16)
+        row = jnp.where(lane == d, listed.astype(jnp.float32), row)
+    info[0] = row
     chosen = [(owner_ref[d] == me).astype(jnp.float32) for d in range(bands)]
 
-    def transform(p):
+    def transform(c):
         halves = []
         for h in range(2):
-            load(p, h).wait()
-            part = raw_ref[:, h * hc + p * width : h * hc + (p + 1) * width]
-            halves.append(mm(gmap, part).reshape(n, mine, width))
-        both[:, :, p * width : (p + 1) * width] = jnp.concatenate(halves, axis=1).astype(
+            load(c, h).wait()
+            at = h * hc + edges[c]
+            halves.append(mm(gmap, raw_ref[:, at : at + cuts[c]]).reshape(n, mine, cuts[c]))
+        both[:, :, edges[c] : edges[c] + cuts[c]] = jnp.concatenate(halves, axis=1).astype(
             jnp.bfloat16
         )
 
-    def span(p, extra=128):
-        return p * width, width + (extra if p == pieces - 1 else 0)
+    def span(p):
+        return starts[p], widths[p]
 
     def remote(source, target, phase, sem, to):
         return pltpu.make_async_remote_copy(
@@ -225,28 +254,30 @@
             device_id={"chan": to}, device_id_type=MESH,
         )
 
-    def copy0(p):
-        cols = pl.ds(*span(p))
+    def copy0(c):
+        cols = pl.ds(edges[c], cuts[c])
         return remote(
             both.at[pl.ds((1 - core) * chips, chips), :, cols], pair.at[:, :, cols],
-            0, rs0.at[p], other,
-        )
-
-    def copy1(p, k):
+            0, rs0.at[c], other,
+        )
+
+    def tell(to, k):
+        return remote(info.at[0], info.at[k], 4, rs4.at[0], to * 2 + core)
+
+    def copy1(p, to, k):
         cols = pl.ds(*span(p))
-        return remote(
-            send1.at[k, :, cols], recv1.at[k, :, cols], 1, rs1.at[p], peer(k) * 2 + core
-        )
-
-    def copy2(p, k):
-        cols = pl.ds(*span(p, 0))
-        return remote(
-            same.at[0, :, cols], same.at[k, :, cols], 2, rs2.at[p], peer(k) * 2 + core
-        )
+        return remote(send1.at[k, :, cols], recv1.at[k, :, cols], 1, rs1.at[p], to * 2 + core)
+
+    def copy2(p, to, k):
+        cols = pl.ds(*span(p))
+        return remote(same.at[0, :, cols], same.at[k, :, cols], 2, rs2.at[p], to * 2 + core)
 
     def copy3(p):
-        cols = pl.ds(*span(p, 0))
+        cols = pl.ds(*span(p))
         return remote(same.at[:, :, cols], cross.at[:, :, cols], 3, rs3.at[p], other)
+
+    def pass_on():
+        return remote(info, info_cross, 5, rs4.at[1], other)
 
     others = pl.ds(1, chips - 1)
 
@@ -255,36 +286,57 @@
         remote(region, region, 1, rs1.at[p], other).wait_recv()
 
     def arrived2(p):
-        region = same.at[others, :, pl.ds(*span(p, 0))]
+        region = same.at[others, :, pl.ds(*span(p))]
         remote(region, region, 2, rs2.at[p], other).wait_recv()
 
-    for p in range(pieces):
-        transform(p)
-    pl.semaphore_wait(barrier, chips)
-    for p in range(pieces):
-        copy0(p).start()
+    @pl.when(core == 0)
+    def _():
+        pl.semaphore_wait(barrier, 1)
+        greet(ready, other)
+
+    for c in range(len(cuts)):
+        transform(c)
+        if c == 0:
+
+            @pl.when(core == 1)
+            def _():
+                pl.semaphore_wait(ready, 1)
+
+        copy0(c).start()
+
+    @pl.when(core == 1)
+    def _():
+        pl.semaphore_wait(barrier, 2 * (chips - 1))
+        greet(ready, other)
+
+    @pl.when(core == 0)
+    def _():
+        pl.semaphore_wait(ready, 1)
+
+    for to, k in first_order:
+        tell(to, k).start()
     for p in range(pieces):
         at, size = span(p)
         cols = slice(at, at + size)
-        copy0(p).wait_recv()
-        for k in order:
-            own = both[core * chips + peer(k), :, cols].astype(jnp.float32)
-            send1[k, :, cols] = (own + pair[peer(k), :, cols].astype(jnp.float32)).astype(
-                jnp.bfloat16
-            )
-            copy1(p, k).start()
+        for c in range(len(cuts)):
+            if at <= edges[c] < at + size:
+                copy0(c).wait_recv()
+        for to, k in first_order:
+            own = both[core * chips + to, :, cols].astype(jnp.float32)
+            send1[k, :, cols] = (own + pair[to, :, cols].astype(jnp.float32)).astype(jnp.bfloat16)
+            copy1(p, to, k).start()
         own = both[core * chips + chip, :, cols].astype(jnp.float32)
         recv1[0, :, cols] = (own + pair[chip, :, cols].astype(jnp.float32)).astype(jnp.bfloat16)
 
     for p in range(pieces):
         arrived1(p)
-        cols = slice(p * width, (p + 1) * width)
+        cols = slice(starts[p], starts[p] + widths[p])
         total = recv1[0, :, cols].astype(jnp.float32)
         for k in range(1, chips):
             total = total + recv1[k, :, cols].astype(jnp.float32)
         squares = total * total
         white = []
-        for b in range(width // block):
+        for b in range(widths[p] // block):
             at = slice(b * block, (b + 1) * block)
             power = jnp.sum(squares[:, at], axis=1, keepdims=True)
             turned = [
@@ -293,44 +345,44 @@
             power = (power + jnp.concatenate(turned, axis=0)) / (2 * block)
             white.append(total[:, at] * lax.rsqrt(power + 1e-06))
         same[0, :, cols] = jnp.concatenate(white, axis=1).astype(jnp.bfloat16)
-        for k in order:
-            copy2(p, k).start()
-
+        for to, k in second_order:
+            copy2(p, to, k).start()
+
+    remote(info.at[others], info.at[others], 4, rs4.at[0], other).wait_recv()
+    pass_on().start()
+    pass_on().wait_recv()
     weights = []
     for i in range(n):
-        weight = jnp.zeros((1, 128), jnp.float32)
+        here = (i % 2 == core).astype(jnp.float32)
+        line = info[peer(i // 2)] * here + info_cross[peer(i // 2)] * (1.0 - here)
+        weight = jnp.zeros((1, 1), jnp.float32)
         for d in range(bands):
-            at = i % 2 * mine + d
-            weight = weight + recv1[peer(i // 2), at : at + 1, hc:].astype(jnp.float32) * chosen[d]
+            weight = weight + line[:, d : d + 1] * chosen[d]
         weights.append(jnp.broadcast_to(weight, (mine, block)))
     scales = [
         jnp.concatenate([weights[t], weights[t + n // 2]], axis=0) for t in range(n // 2)
     ]
 
-    def products(held):
-        held = held.astype(jnp.float32)
-        tiles = [held[:, t * block : (t + 1) * block] for t in range(n // 2)]
-        left = [tiles[t] * scales[t] for t in range(n // 2)]
-        for d in range(bands):
-            tiles.append(
-                jnp.concatenate([tiles[d][mine:], jnp.zeros((mine, block), jnp.float32)], axis=0)
-            )
-        right = []
-        for t in range(n // 2):
-            tile = tiles[t + 1] * chosen[0]
-            for d in range(1, bands):
-                tile = tile + tiles[t + d + 1] * chosen[d]
-            right.append(tile)
-        return left, right
-
-    def add(total, refs):
+    scales = [scale.astype(jnp.bfloat16) for scale in scales]
+    picks = [jnp.full((2 * mine, block), pick, jnp.float32).astype(jnp.bfloat16) for pick in chosen]
+
+    def add(total, held):
         lefts, rights = [], []
-        for held in refs:
-            left, right = products(held)
-            lefts += left
-            rights += right
-        left = jnp.concatenate(lefts, axis=0).astype(jnp.bfloat16)
-        right = jnp.concatenate(rights, axis=0).astype(jnp.bfloat16)
+        for k in range(chips):
+            tiles = [held[k, :, t * block : (t + 1) * block] for t in range(n // 2)]
+            lefts += [tiles[t] * scales[t] for t in range(n // 2)]
+            for d in range(bands):
+                later = tiles[d].astype(jnp.float32)[mine:]
+                tiles.append(
+                    jnp.concatenate([later, jnp.zeros_like(later)], axis=0).astype(jnp.bfloat16)
+                )
+            for t in range(n // 2):
+                tile = tiles[t + 1] * picks[0]
+                for d in range(1, bands):
+                    tile = tile + tiles[t + d + 1] * picks[d]
+                rights.append(tile)
+        left = jnp.concatenate(lefts, axis=0)
+        right = jnp.concatenate(rights, axis=0)
         return total + lax.dot_general(
             left, right, (((0,), (0,)), ((), ())), preferred_element_type=jnp.float32
         )
@@ -338,19 +390,18 @@
     for p in range(pieces):
         arrived2(p)
         copy3(p).start()
-    result = jnp.zeros((block, block), jnp.float32)
-    for k in range(0, chips, 2):
-        result = add(result, [same[k], same[k + 1]])
+    result = add(jnp.zeros((block, block), jnp.float32), same)
     for p in range(pieces):
         copy3(p).wait_recv()
-    for k in range(0, chips, 2):
-        result = add(result, [cross[k], cross[k + 1]])
+    result = add(result, cross)
     out_ref[0] = result * (1.0 / (2 * bins))
 
     remote(pair, pair, 0, rs0.at[0], other).wait_send()
     remote(recv1.at[others], recv1.at[others], 1, rs0.at[0], other).wait_send()
     remote(same.at[others], same.at[others], 2, rs0.at[0], other).wait_send()
     remote(same, same, 3, rs0.at[0], other).wait_send()
+    remote(info.at[others], info.at[others], 4, rs0.at[0], other).wait_send()
+    remote(info, info, 5, rs0.at[0], other).wait_send()
 
 
 def fused(raw, taps, tile_dist, tile_count, owner):
@@ -362,12 +413,14 @@
     mine = 2 * (steps * n // 16) // n
     chips = n // 2
     hc = channels // 2
-    pieces = 4
+    widths = [hc * k // 8 for k in (4,4,)]
+    cuts = [hc * k // 8 for k in (4,4,)]
+    pieces = len(widths)
     vmem, hbm = pl.BlockSpec(memory_space=pltpu.VMEM), pl.BlockSpec(memory_space=pltpu.HBM)
     dma = pltpu.SemaphoreType.DMA
     held = functools.partial(pltpu.with_memory_space_constraint, memory_space=pltpu.HBM)
     return pl.pallas_call(
-        functools.partial(fused_kernel, n, bands, pieces),
+        functools.partial(fused_kernel, n, bands, widths, cuts),
         out_shape=jax.ShapeDtypeStruct((1, block, block), jnp.float32),
         in_specs=[hbm] * 5,
         out_specs=vmem,
@@ -377,19 +430,23 @@
             pltpu.SMEM(tile_dist.shape, jnp.int32),
             pltpu.SMEM(tile_count.shape, jnp.int32),
             pltpu.SMEM(owner.shape, jnp.int32),
-            dma((2 * pieces,)),
+            dma((2 * len(cuts),)),
             dma((4,)),
-            pltpu.VMEM((n, 2 * mine, hc + 128), jnp.bfloat16),
-            pltpu.VMEM((chips, 2 * mine, hc + 128), jnp.bfloat16),
-            pltpu.VMEM((chips, 2 * mine, hc + 128), jnp.bfloat16),
-            pltpu.VMEM((chips, 2 * mine, hc + 128), jnp.bfloat16),
+            pltpu.VMEM((n, 2 * mine, hc), jnp.bfloat16),
             pltpu.VMEM((chips, 2 * mine, hc), jnp.bfloat16),
             pltpu.VMEM((chips, 2 * mine, hc), jnp.bfloat16),
-            dma((4,)),
+            pltpu.VMEM((chips, 2 * mine, hc), jnp.bfloat16),
+            pltpu.VMEM((chips, 2 * mine, hc), jnp.bfloat16),
+            pltpu.VMEM((chips, 2 * mine, hc), jnp.bfloat16),
+            pltpu.SemaphoreType.REGULAR,
+            pltpu.VMEM((chips, 1, 128), jnp.float32),
+            pltpu.VMEM((chips, 1, 128), jnp.float32),
+            dma((6,)),
+            dma((len(cuts),)),
             dma((pieces,)),
             dma((pieces,)),
             dma((pieces,)),
-            dma((pieces,)),
+            dma((2,)),
         ],
         compiler_params=pltpu.CompilerParams(
             collective_id=0, has_side_effects=True, vmem_limit_bytes=int(53.25 * 2**20)

time: 25 us -> 22.2 us (0.89)
  Pallas kernels: 23.5 us -> 20.7 us
    pallas_call x1, Pallas kernels: 23.5 us -> 20.7 us  [fused(): pl.pallas_call(functools.partial(fused_kernel, n, bands, widths, cuts), o...]
where the time goes in v3:
time: 22.2 us; the launch traced here: 22 us
  Pallas kernels  20.7 us (93%)
  between operations  0.66 us (3%)
  local copies, waits for them, and re-layouts  0.63 us (3%)
    pallas_call x1, Pallas kernels, fused(): pl.pallas_call(functools.partial(fused_kernel, n, bands, widths, cuts), o...  20.7 us
    unnamed x1, local copies, waits for them, and re-layouts  0.63 us

profile of v3, /device:TPU:1, one launch (start us, length us, event | category | flops | bytes accessed | tf_op | source)
XLA Modules:
  0.0 22.0 jit_solution(10156160407739671838)
XLA Ops:
  0.7 20.7 %shard_map.55 = f32[1,128,128]{2,1,0:T(8,128)S(1)} custom-call(bf16[320,2048]{1,0:T(8,128)(2,1)} %raw_hbm.1, bf16[255]{0:T(256)(128)(2,1)} %taps_hbm.1, s32[1,4]{1,0:T(1,128)} %dist_hbm.1, s32[1]{0:T(128)S(6)} %copy.7.count_hbm, s32[4]{0:T(128)} %owner_hbm.1), custom_call_target="tpu_custom_call" | custom-call | tf_op jit(solution)/shard_map/pallas_call | solution.py:422
  21.4 0.6 %copy.8 = f32[1,128,128]{2,1,0:T(8,128)} copy(f32[1,128,128]{2,1,0:T(8,128)S(1)} %shard_map.55) | data formatting | bytes 131072

commit v4 on v3

v4 whole, which is shorter than its diff:
```python
import functools
import math

import jax
import jax.numpy as jnp
from jax import lax
from jax.experimental import pallas as pl
from jax.experimental.pallas import tpu as pltpu
from jax.sharding import PartitionSpec as P
import numpy as np

MESH = pl.DeviceIdType.MESH


def extended(x, sides, width):
    for axis, dim in sides:
        size, length = (lax.axis_size(axis), x.shape[dim])
        up = [(i, (i + 1) % size) for i in range(size - 1)]
        down = [(j, i) for i, j in up]
        last = lax.slice_in_dim(x, length - width, length, axis=dim)
        initial = lax.slice_in_dim(x, 0, width, axis=dim)
        before = lax.ppermute(last, axis, up)
        after = lax.ppermute(initial, axis, down)
        x = jnp.concatenate([before, x, after], axis=dim)
    return x


def passed_along(x, axis, by):
    size = lax.axis_size(axis)
    pairs = [(i, i + by) for i in range(size) if 0 <= i + by < size]
    return lax.ppermute(x, axis, pairs)


def band_matrix(taps, out_rows, in_cols):
    period = in_cols + 5
    padded = jnp.pad(taps, (0, period - taps.shape[0]))
    return jnp.tile(padded, out_rows)[: out_rows * in_cols].reshape(out_rows, in_cols)


def whiten(block):
    length, channels = block.shape
    bins = length // 16
    freqs = jnp.arange(1, bins + 1, dtype=jnp.int32)[:, None]
    times = jnp.arange(length, dtype=jnp.int32)[None, :]
    angle = (freqs * times % length).astype(jnp.float32) * (2.0 * math.pi / length)
    table = jnp.concatenate([jnp.cos(angle), -jnp.sin(angle)], axis=0)
    table_high = table.astype(jnp.bfloat16)
    table_low = (table - table_high.astype(jnp.float32)).astype(jnp.bfloat16)
    spectrum = jnp.dot(table_high, block, preferred_element_type=jnp.float32)
    spectrum = spectrum + jnp.dot(table_low, block, preferred_element_type=jnp.float32)
    squares = spectrum * spectrum
    power = jnp.sum(squares[:bins] + squares[bins:], axis=1) / (2 * channels)
    gain = lax.rsqrt(power + 1e-06)
    return (spectrum * jnp.concatenate([gain, gain])[:, None]).astype(jnp.bfloat16)


def cross_tile(mine, partner, scale):
    product = lax.dot_general(
        mine, partner, (((0,), (0,)), ((), ())), preferred_element_type=jnp.float32
    )
    return product * scale


def streamed(raw, taps, tile_dist, tile_count, owner):
    rows = raw.shape[0]
    width = taps.shape[0]
    half = (width - 1) // 2
    out_rows = rows // 5
    banded = band_matrix(taps, out_rows, rows + 2 * half)
    padded = extended(raw, (("chan", 0),), half)
    filtered = jnp.dot(banded, padded, preferred_element_type=jnp.float32)
    decimated = filtered.astype(jnp.bfloat16)
    regrouped = lax.all_to_all(decimated, "chan", split_axis=1, concat_axis=0, tiled=True)
    whitened = whiten(regrouped)
    channels = whitened.shape[1]
    scale = 1.0 / whitened.shape[0]
    bands = tile_dist.shape[1]
    slots = jnp.arange(bands, dtype=jnp.int32) < tile_count[0]
    stacks = []
    for distance in range(1, bands + 1):
        partner = passed_along(whitened, "chan", -distance)
        listed = jnp.sum(((tile_dist[0] == distance) & slots).astype(jnp.int32))
        tile = lax.cond(
            listed > 0,
            lambda first, second: cross_tile(first, second, scale),
            lambda first, second: jnp.zeros((channels, channels), jnp.float32),
            whitened,
            partner,
        )
        stacks.append(tile)
    stacked = jnp.stack(stacks)
    totals = lax.psum(stacked, "chan")
    selected = (owner == lax.axis_index("chan")).astype(jnp.float32)
    return jnp.einsum("b,bxy->xy", selected, totals, precision=lax.Precision.HIGHEST)[None]


def split(x):
    high = x.astype(jnp.bfloat16)
    low = (x - high.astype(jnp.float32)).astype(jnp.bfloat16)
    return high, low


def mm(a, b):
    return jnp.dot(a, b, preferred_element_type=jnp.float32)


def window_factors(steps, lead, length, bins, reach, rank):
    width = 2 * steps + 2 * lead
    chips = length // (2 * steps)
    freq = np.arange(1, bins + 1)[:, None]
    low, high = -(reach // 5), 2 * steps + (reach - 1) // 5 + 1
    time = np.arange(low, high)[None, :]

    def table(chip):
        angle = 2.0 * np.pi * ((freq * (time + 2 * steps * chip)) % length) / length
        return np.concatenate([np.cos(angle), -np.sin(angle)], axis=0)

    basis = np.linalg.svd(table(0), full_matrices=False)[2][:rank]
    lefts = np.stack([basis @ table(chip).T for chip in range(chips)])
    padded = np.zeros((rank, width))
    padded[:, lead + low : lead + high] = basis
    rights = np.stack([padded[:, c * steps : (c + 1) * steps + 2 * lead] for c in range(2)])
    return lefts.astype(np.float32), rights.astype(np.float32)


def fused_kernel(
    n, bands,
    raw_hbm, taps_hbm, dist_hbm, count_hbm, owner_hbm, left_hbm, right_hbm, out_ref,
    raw_ref, taps_ref, dist_ref, count_ref, owner_ref, left_ref, right_ref, loads, smalls,
    joined, both, pair, send1, recv1, gath, ready, info, info_cross, sent, rs0, rs1, rs2, rs3, rs4,
):
    me = lax.axis_index("chan")
    chips = n // 2
    chip, core = me // 2, me % 2
    other = chip * 2 + 1 - core
    rows, channels = raw_ref.shape
    rank = right_ref.shape[0]
    block = channels // n
    steps = rows // 5
    length = steps * n
    bins = length // 16
    window = right_ref.shape[1]
    lead = (window - steps) // 2
    half = (taps_hbm.shape[0] - 1) // 2
    lanes = 1024
    start = lanes - 5 * lead - half
    cuts = 2
    cut = channels // cuts

    z, y = chip // 2, chip % 2

    def peer(k):
        far = [z, z + 1 - 2 * (z % 2), lax.rem(z + 2, 4), 3 - z][k // 2]
        return far * 2 + (1 - y if k % 2 else y)

    def slot(to):
        low = y + to % 2 - 2 * y * (to % 2)
        mid = z % 2 + to // 2 % 2 - 2 * (z % 2) * (to // 2 % 2)
        high = z // 2 + to // 4 - 2 * (z // 2) * (to // 4)
        return 4 * high + 2 * mid + low

    first_order = [(peer(k), k) for k in (7, 6, 5, 4, 3, 2, 1)]
    rising = [k + (k >= chip).astype(jnp.int32) for k in range(chips - 1)]
    second_order = [(to, slot(to)) for to in rising]

    barrier = pltpu.get_barrier_semaphore()

    def greet(semaphore, to):
        pl.semaphore_signal(semaphore, inc=1, device_id={"chan": to}, device_id_type=MESH)

    @pl.when(core == 1)
    def _():
        greet(barrier, other)

    for k in range(chips - 1, 0, -1):
        greet(barrier, peer(k) * 2 + 1)

    small = [
        pltpu.make_async_copy(source, held, smalls.at[at])
        for at, (source, held) in enumerate(
            [
                (taps_hbm, taps_ref),
                (right_hbm.at[core], right_ref),
                (dist_hbm, dist_ref),
                (count_hbm, count_ref),
                (owner_hbm, owner_ref),
                (left_hbm, left_ref),
            ]
        )
    ]
    for load in small[:2]:
        load.start()

    def load(c):
        cols = pl.ds(c * cut, cut)
        return pltpu.make_async_copy(raw_hbm.at[:, cols], raw_ref.at[:, cols], loads.at[c])

    for c in range(cuts):
        load(c).start()
    for load_one in small[2:]:
        load_one.start()

    for load_one in small[:2]:
        load_one.wait()
    tap = taps_ref[...].astype(jnp.float32).reshape(1, -1)
    line = jnp.concatenate(
        [
            jnp.zeros((1, start), jnp.float32),
            tap,
            jnp.zeros((1, lanes - start - tap.shape[1]), jnp.float32),
        ],
        axis=1,
    )
    first = pltpu.roll(jnp.broadcast_to(line, (8, lanes)), 0, 1, stride=5, stride_axis=0)
    banded = jnp.concatenate(
        [pltpu.roll(first, 40 * q, 1)[:, :384] for q in range(window // 8)], axis=0
    ).astype(jnp.bfloat16)[:, :rows]
    time = me * steps - lead + lax.broadcasted_iota(jnp.int32, (rank, window), 1)
    table = jnp.where((time >= 0) & (time < length), right_ref[...], 0.0)
    table_high, table_low = split(table)
    gmap = (mm(table_high, banded) + mm(table_low, banded)).astype(jnp.bfloat16)

    def transform(c):
        load(c).wait()
        part = mm(gmap, raw_ref[:, c * cut : (c + 1) * cut]).astype(jnp.bfloat16)
        for j in range(cut // block):
            at = c * (cut // block) + j
            both[at % 2 * chips + at // 2] = part[:, j * block : (j + 1) * block]

    def remote(source, target, phase, sem, to):
        return pltpu.make_async_remote_copy(
            src_ref=source, dst_ref=target, send_sem=sent.at[phase], recv_sem=sem,
            device_id={"chan": to}, device_id_type=MESH,
        )

    def copy0(c):
        few = chips // cuts
        return remote(
            both.at[pl.ds((1 - core) * chips + c * few, few)], pair.at[pl.ds(c * few, few)],
            0, rs0.at[c], other,
        )

    def tell(to, k):
        return remote(info.at[0], info.at[k], 4, rs4.at[0], to * 2 + core)

    def pass_on():
        return remote(info, info_cross, 5, rs4.at[1], other)

    def copy1(to, k):
        return remote(send1.at[k], recv1.at[k], 1, rs1, to * 2 + core)

    groups = [(0, chips // 2), (chips // 2, chips)]

    def copy2(to, k, g):
        return remote(gath.at[0, 0], gath.at[0, k], 2, rs2.at[g], to * 2 + core)

    def copy3(g):
        first, last = groups[g]
        some = pl.ds(first, last - first)
        return remote(gath.at[0, some], gath.at[1, some], 3, rs3.at[g], other)

    others = pl.ds(1, chips - 1)

    @pl.when(core == 0)
    def _():
        pl.semaphore_wait(barrier, 1)
        greet(ready, other)

    for c in range(cuts):
        transform(c)
        if c == 0:

            @pl.when(core == 1)
            def _():
                pl.semaphore_wait(ready, 1)

        copy0(c).start()

    for load_one in small[2:]:
        load_one.wait()
    lane = lax.broadcasted_iota(jnp.int32, (1, 128), 1)
    row = jnp.zeros((1, 128), jnp.float32)
    for d in range(bands):
        listed = jnp.int32(0)
        for s in range(bands):
            hit = (dist_ref[0, s] == d + 1) & (s < count_ref[0])
            listed = listed + hit.astype(jnp.int32)
        row = jnp.where(lane == d, listed.astype(jnp.float32), row)
    info[0] = row
    chosen = [(owner_ref[d] == me).astype(jnp.int32) for d in range(bands)]
    shift = sum((d + 1) * chosen[d] for d in range(bands))
    joined[...] = jnp.transpose(
        jnp.concatenate([left_ref[peer(k)] for k in range(chips)], axis=0)
    ).astype(jnp.bfloat16)

    @pl.when(core == 1)
    def _():
        pl.semaphore_wait(barrier, 2 * (chips - 1))
        greet(ready, other)

    @pl.when(core == 0)
    def _():
        pl.semaphore_wait(ready, 1)

    for c in range(cuts):
        copy0(c).wait_recv()
    for to, k in first_order:
        own = both[core * chips + to].astype(jnp.float32)
        send1[k] = (own + pair[to].astype(jnp.float32)).astype(jnp.bfloat16)
        copy1(to, k).start()
    own = both[core * chips + chip].astype(jnp.float32)
    recv1[0] = (own + pair[chip].astype(jnp.float32)).astype(jnp.bfloat16)
    for to, k in first_order:
        tell(to, k).start()

    remote(recv1.at[others], recv1.at[others], 1, rs1, other).wait_recv()
    spectrum = mm(joined[...], recv1[...].reshape(chips * rank, block))
    power = jnp.sum(spectrum * spectrum, axis=1, keepdims=True)
    power = (power[:bins] + power[bins:]) / (2 * block)
    gain = lax.rsqrt(power + 1e-06)
    gath[0, 0] = (spectrum * jnp.concatenate([gain, gain], axis=0)).astype(jnp.bfloat16)
    for to, k in second_order:
        copy2(to, k, k // (chips // 2)).start()

    remote(info.at[others], info.at[others], 4, rs4.at[0], other).wait_recv()
    pass_on().start()
    pass_on().wait_recv()
    weights = []
    for i in range(n):
        here = ((i + core) % 2 == 0).astype(jnp.float32)
        line = info[peer(i // 2)] * here + info_cross[peer(i // 2)] * (1.0 - here)
        weight = jnp.zeros((1, 1), jnp.float32)
        for d in range(bands):
            weight = weight + line[:, d : d + 1] * chosen[d].astype(jnp.float32)
        weights.append(jnp.broadcast_to(weight, (block, block)).astype(jnp.bfloat16))

    for g, (first, last) in enumerate(groups):
        low = max(first, 1)
        if last > low:
            some = gath.at[0, pl.ds(low, last - low)]
            remote(some, some, 2, rs2.at[g], other).wait_recv()
        copy3(g).start()
    for g in range(len(groups)):
        copy3(g).wait_recv()
    lefts, rights = [], []
    for i in range(n - 1):
        lefts.append(gath[(i + core) % 2, slot(i // 2)] * weights[i])
        later = jnp.minimum(i + shift, n - 1)
        rights.append(gath[(later + core) % 2, slot(later // 2)])
    result = lax.dot_general(
        jnp.concatenate(lefts, axis=0), jnp.concatenate(rights, axis=0),
        (((0,), (0,)), ((), ())), preferred_element_type=jnp.float32,
    )
    out_ref[0] = result * (1.0 / (2 * bins))

    remote(pair, pair, 0, rs0.at[0], other).wait_send()
    remote(recv1.at[others], recv1.at[others], 1, rs0.at[0], other).wait_send()
    remote(gath.at[0, others], gath.at[0, others], 2, rs0.at[0], other).wait_send()
    remote(gath.at[0], gath.at[0], 3, rs0.at[0], other).wait_send()
    remote(info.at[others], info.at[others], 4, rs0.at[0], other).wait_send()
    remote(info, info, 5, rs0.at[0], other).wait_send()


def fused(raw, taps, tile_dist, tile_count, owner):
    n = lax.axis_size("chan")
    rows, channels = raw.shape
    bands = tile_dist.shape[1]
    block = channels // n
    steps = rows // 5
    chips = n // 2
    rank = 48
    lead = (128 - steps) // 2
    lefts, rights = window_factors(
        steps, lead, steps * n, steps * n // 16, (taps.shape[0] - 1) // 2, rank
    )
    vmem, hbm = pl.BlockSpec(memory_space=pltpu.VMEM), pl.BlockSpec(memory_space=pltpu.HBM)
    dma = pltpu.SemaphoreType.DMA
    held = functools.partial(pltpu.with_memory_space_constraint, memory_space=pltpu.HBM)
    return pl.pallas_call(
        functools.partial(fused_kernel, n, bands),
        out_shape=jax.ShapeDtypeStruct((1, block, block), jnp.float32),
        in_specs=[hbm] * 7,
        out_specs=vmem,
        scratch_shapes=[
            pltpu.VMEM(raw.shape, raw.dtype),
            pltpu.VMEM(taps.shape, taps.dtype),
            pltpu.SMEM(tile_dist.shape, jnp.int32),
            pltpu.SMEM(tile_count.shape, jnp.int32),
            pltpu.SMEM(owner.shape, jnp.int32),
            pltpu.VMEM(lefts.shape, jnp.float32),
            pltpu.VMEM(rights.shape[1:], jnp.float32),
            dma((2,)),
            dma((6,)),
            pltpu.VMEM((lefts.shape[2], chips * rank), jnp.bfloat16),
            pltpu.VMEM((n, rank, block), jnp.bfloat16),
            pltpu.VMEM((chips, rank, block), jnp.bfloat16),
            pltpu.VMEM((chips, rank, block), jnp.bfloat16),
            pltpu.VMEM((chips, rank, block), jnp.bfloat16),
            pltpu.VMEM((2, chips, block, block), jnp.bfloat16),
            pltpu.SemaphoreType.REGULAR,
            pltpu.VMEM((chips, 1, 128), jnp.float32),
            pltpu.VMEM((chips, 1, 128), jnp.float32),
            dma((6,)),
            dma((2,)),
            dma,
            dma((2,)),
            dma((2,)),
            dma((2,)),
        ],
        compiler_params=pltpu.CompilerParams(
            collective_id=0, has_side_effects=True, vmem_limit_bytes=int(53.25 * 2**20)
        ),
    )(held(raw), held(taps), held(tile_dist), tile_count, held(owner), held(jnp.asarray(lefts)), held(jnp.asarray(rights)))


def shards(raw, taps, tile_dist, tile_count, owner):
    n = lax.axis_size("chan")
    rows, channels = raw.shape
    steps = rows // 5
    fits = (
        channels == 128 * n
        and n == 16
        and rows == 320
        and taps.shape[0] == 255
        and tile_dist.shape[1] == 4
    )
    path = fused if fits else streamed
    return path(raw, taps, tile_dist, tile_count, owner)


def solution(mesh):
    in_specs = (P("chan", "groups"), P(), P("chan", "groups"), P(("groups", "chan")), P("groups"))
    out_specs = P("chan", "groups", None)
    return jax.shard_map(shards, mesh=mesh, in_specs=in_specs, out_specs=out_specs, check_vma=False)
```

time: 22.2 us -> 19.8 us (0.89)
  Pallas kernels: 20.7 us -> 18.3 us
    pallas_call x1, Pallas kernels: 20.7 us -> 18.3 us  [fused(): pl.pallas_call(functools.partial(fused_kernel, n, bands), out_shape=jax.S...]
where the time goes in v4:
time: 19.8 us; the launch traced here: 19.6 us
  Pallas kernels  18.3 us (92%)
  between operations  0.66 us (3%)
  local copies, waits for them, and re-layouts  0.63 us (3%)
    pallas_call x1, Pallas kernels, fused(): pl.pallas_call(functools.partial(fused_kernel, n, bands), out_shape=jax.S...  18.3 us
    unnamed x1, local copies, waits for them, and re-layouts  0.63 us

profile of v4, /device:TPU:1, one launch (start us, length us, event | category | flops | bytes accessed | tf_op | source)
XLA Modules:
  0.0 19.6 jit_solution(18332907706451733648)
XLA Ops:
  0.7 18.3 %shard_map.73 = f32[1,128,128]{2,1,0:T(8,128)S(1)} custom-call(bf16[320,2048]{1,0:T(8,128)(2,1)} %raw_hbm.1, bf16[255]{0:T(256)(128)(2,1)} %taps_hbm.1, s32[1,4]{1,0:T(1,128)} %dist_hbm.1, s32[1]{0:T(128)S(6)} %copy.9.count_hbm, s32[4]{0:T(128)} %owner_hbm.1, f32[8,48,128]{2,1,0:T(8,128)} %constant.4.clone.left_hbm, f32[2,48,128]{2,1,0:T(8,128)} %constant.5.clone.right_hbm), custom_call_target="tpu_custom_call" | custom-call | tf_op jit(solution)/shard_map/pallas_call | solution.py:379
  19.0 0.6 %copy.10 = f32[1,128,128]{2,1,0:T(8,128)} copy(f32[1,128,128]{2,1,0:T(8,128)S(1)} %shard_map.73) | data formatting | bytes 131072

commit v5 on v4

--- a/solution.py
+++ b/solution.py
@@ -124,10 +124,10 @@
 
 
 def fused_kernel(
-    n, bands,
+    n, bands, kept,
     raw_hbm, taps_hbm, dist_hbm, count_hbm, owner_hbm, left_hbm, right_hbm, out_ref,
     raw_ref, taps_ref, dist_ref, count_ref, owner_ref, left_ref, right_ref, loads, smalls,
-    joined, both, pair, send1, recv1, gath, ready, info, info_cross, sent, rs0, rs1, rs2, rs3, rs4,
+    joined, both, pair, send1, recv1, gath, turned, ready, sent, rs0, rs1, rs2, rs3,
 ):
     me = lax.axis_index("chan")
     chips = n // 2
@@ -159,10 +159,6 @@
         high = z // 2 + to // 4 - 2 * (z // 2) * (to // 4)
         return 4 * high + 2 * mid + low
 
-    first_order = [(peer(k), k) for k in (7, 6, 5, 4, 3, 2, 1)]
-    rising = [k + (k >= chip).astype(jnp.int32) for k in range(chips - 1)]
-    second_order = [(to, slot(to)) for to in rising]
-
     barrier = pltpu.get_barrier_semaphore()
 
     def greet(semaphore, to):
@@ -172,8 +168,11 @@
     def _():
         greet(barrier, other)
 
-    for k in range(chips - 1, 0, -1):
-        greet(barrier, peer(k) * 2 + 1)
+    for q in range(chips):
+
+        @pl.when(chip != q)
+        def _():
+            greet(barrier, q * 2 + 1)
 
     small = [
         pltpu.make_async_copy(source, held, smalls.at[at])
@@ -188,7 +187,7 @@
             ]
         )
     ]
-    for load in small[:2]:
+    for load in small[:4]:
         load.start()
 
     def load(c):
@@ -197,7 +196,7 @@
 
     for c in range(cuts):
         load(c).start()
-    for load_one in small[2:]:
+    for load_one in small[4:]:
         load_one.start()
 
     for load_one in small[:2]:
@@ -220,12 +219,26 @@
     table_high, table_low = split(table)
     gmap = (mm(table_high, banded) + mm(table_low, banded)).astype(jnp.bfloat16)
 
+    for load_one in small[2:4]:
+        load_one.wait()
+    line = lax.broadcasted_iota(jnp.int32, (rank, block), 0)
+    lane = lax.broadcasted_iota(jnp.int32, (rank, block), 1)
+    info = jnp.zeros((rank, block), jnp.float32)
+    for d in range(bands):
+        listed = jnp.int32(0)
+        for s in range(bands):
+            hit = (dist_ref[0, s] == d + 1) & (s < count_ref[0])
+            listed = listed + hit.astype(jnp.int32)
+        info = jnp.where((line == kept + core) & (lane == d), listed.astype(jnp.float32), info)
+
     def transform(c):
         load(c).wait()
-        part = mm(gmap, raw_ref[:, c * cut : (c + 1) * cut]).astype(jnp.bfloat16)
+        part = mm(gmap, raw_ref[:, c * cut : (c + 1) * cut])
         for j in range(cut // block):
             at = c * (cut // block) + j
-            both[at % 2 * chips + at // 2] = part[:, j * block : (j + 1) * block]
+            both[at % 2 * chips + at // 2] = (
+                part[:, j * block : (j + 1) * block] + info
+            ).astype(jnp.bfloat16)
 
     def remote(source, target, phase, sem, to):
         return pltpu.make_async_remote_copy(
@@ -240,24 +253,14 @@
             0, rs0.at[c], other,
         )
 
-    def tell(to, k):
-        return remote(info.at[0], info.at[k], 4, rs4.at[0], to * 2 + core)
-
-    def pass_on():
-        return remote(info, info_cross, 5, rs4.at[1], other)
-
-    def copy1(to, k):
-        return remote(send1.at[k], recv1.at[k], 1, rs1, to * 2 + core)
-
-    groups = [(0, chips // 2), (chips // 2, chips)]
-
-    def copy2(to, k, g):
-        return remote(gath.at[0, 0], gath.at[0, k], 2, rs2.at[g], to * 2 + core)
-
-    def copy3(g):
-        first, last = groups[g]
-        some = pl.ds(first, last - first)
-        return remote(gath.at[0, some], gath.at[1, some], 3, rs3.at[g], other)
+    def copy1(q):
+        return remote(send1.at[q], recv1.at[slot(q)], 1, rs1, q * 2 + core)
+
+    def copy2(source, to):
+        return remote(gath.at[source], gath.at[source], 2, rs2.at[source], to * 2 + core)
+
+    def copy3(q):
+        return remote(gath.at[q], gath.at[chips + q], 3, rs3.at[q], other)
 
     others = pl.ds(1, chips - 1)
 
@@ -276,89 +279,97 @@
 
         copy0(c).start()
 
-    for load_one in small[2:]:
+    @pl.when(core == 1)
+    def _():
+
+        pl.semaphore_wait(barrier, 2 * (chips - 1))
+        greet(ready, other)
+
+    @pl.when(core == 0)
+    def _():
+        pl.semaphore_wait(ready, 1)
+
+    for c in range(cuts):
+        copy0(c).wait_recv()
+    for q in range(chips - 1, -1, -1):
+        own = both[core * chips + q].astype(jnp.float32)
+        send1[q] = (own + pair[q].astype(jnp.float32)).astype(jnp.bfloat16)
+
+        @pl.when(chip != q)
+        def _():
+            copy1(q).start()
+
+    for load_one in small[4:]:
         load_one.wait()
-    lane = lax.broadcasted_iota(jnp.int32, (1, 128), 1)
-    row = jnp.zeros((1, 128), jnp.float32)
-    for d in range(bands):
-        listed = jnp.int32(0)
-        for s in range(bands):
-            hit = (dist_ref[0, s] == d + 1) & (s < count_ref[0])
-            listed = listed + hit.astype(jnp.int32)
-        row = jnp.where(lane == d, listed.astype(jnp.float32), row)
-    info[0] = row
     chosen = [(owner_ref[d] == me).astype(jnp.int32) for d in range(bands)]
     shift = sum((d + 1) * chosen[d] for d in range(bands))
     joined[...] = jnp.transpose(
         jnp.concatenate([left_ref[peer(k)] for k in range(chips)], axis=0)
     ).astype(jnp.bfloat16)
 
-    @pl.when(core == 1)
-    def _():
-        pl.semaphore_wait(barrier, 2 * (chips - 1))
-        greet(ready, other)
-
-    @pl.when(core == 0)
-    def _():
-        pl.semaphore_wait(ready, 1)
-
-    for c in range(cuts):
-        copy0(c).wait_recv()
-    for to, k in first_order:
-        own = both[core * chips + to].astype(jnp.float32)
-        send1[k] = (own + pair[to].astype(jnp.float32)).astype(jnp.bfloat16)
-        copy1(to, k).start()
-    own = both[core * chips + chip].astype(jnp.float32)
-    recv1[0] = (own + pair[chip].astype(jnp.float32)).astype(jnp.bfloat16)
-    for to, k in first_order:
-        tell(to, k).start()
-
+
+    tops = kept // 16 * 16
+
+    recv1[0] = send1[chip]
     remote(recv1.at[others], recv1.at[others], 1, rs1, other).wait_recv()
     spectrum = mm(joined[...], recv1[...].reshape(chips * rank, block))
     power = jnp.sum(spectrum * spectrum, axis=1, keepdims=True)
     power = (power[:bins] + power[bins:]) / (2 * block)
     gain = lax.rsqrt(power + 1e-06)
-    gath[0, 0] = (spectrum * jnp.concatenate([gain, gain], axis=0)).astype(jnp.bfloat16)
-    for to, k in second_order:
-        copy2(to, k, k // (chips // 2)).start()
-
-    remote(info.at[others], info.at[others], 4, rs4.at[0], other).wait_recv()
-    pass_on().start()
-    pass_on().wait_recv()
-    weights = []
-    for i in range(n):
-        here = ((i + core) % 2 == 0).astype(jnp.float32)
-        line = info[peer(i // 2)] * here + info_cross[peer(i // 2)] * (1.0 - here)
+    gath[chip] = (spectrum * jnp.concatenate([gain, gain], axis=0)).astype(jnp.bfloat16)
+    for q in (*range(0, chips, 2), *range(1, chips, 2)):
+
+        @pl.when(chip != q)
+        def _():
+            copy2(chip, q).start()
+
+    picks = [pick.astype(jnp.float32) for pick in chosen]
+    first_core = (core == 0).astype(jnp.float32)
+
+    def weigh(rel, p):
+        lines = recv1[slot(p), tops:].astype(jnp.float32)
+        pair_lines = [lines[kept - tops + c : kept - tops + c + 1] for c in range(2)]
+        own = pair_lines[rel] * first_core + pair_lines[1 - rel] * (1.0 - first_core)
         weight = jnp.zeros((1, 1), jnp.float32)
         for d in range(bands):
-            weight = weight + line[:, d : d + 1] * chosen[d].astype(jnp.float32)
-        weights.append(jnp.broadcast_to(weight, (block, block)).astype(jnp.bfloat16))
-
-    for g, (first, last) in enumerate(groups):
-        low = max(first, 1)
-        if last > low:
-            some = gath.at[0, pl.ds(low, last - low)]
-            remote(some, some, 2, rs2.at[g], other).wait_recv()
-        copy3(g).start()
-    for g in range(len(groups)):
-        copy3(g).wait_recv()
-    lefts, rights = [], []
-    for i in range(n - 1):
-        lefts.append(gath[(i + core) % 2, slot(i // 2)] * weights[i])
-        later = jnp.minimum(i + shift, n - 1)
-        rights.append(gath[(later + core) % 2, slot(later // 2)])
-    result = lax.dot_general(
-        jnp.concatenate(lefts, axis=0), jnp.concatenate(rights, axis=0),
-        (((0,), (0,)), ((), ())), preferred_element_type=jnp.float32,
-    )
+            weight = weight + own[:, d : d + 1] * picks[d]
+        return jnp.broadcast_to(weight, (block, block)).astype(jnp.bfloat16)
+
+    for q in range(chips):
+
+        @pl.when(chip != q)
+        def _():
+            copy2(q, q).wait_recv()
+
+        copy3(q).start()
+
+    weights = [[weigh(rel, p) for p in range(chips)] for rel in range(2)]
+
+    def turn(rel, first, last):
+        tiles = [gath[rel * chips + u] * weights[rel][u] for u in range(first, last)]
+        at = (rel * chips + first) * block
+        turned[:, at : at + (last - first) * block] = jnp.transpose(
+            jnp.concatenate(tiles, axis=0)
+        )
+
+    turn(0, 0, chips)
+    for q in range(chips):
+        copy3(q).wait_recv()
+        turn(1, q, q + 1)
+    rights = []
+    for rel in range(2):
+        for k in range(chips):
+            later = jnp.minimum(k * 2 + (core + rel) % 2 + shift, n - 1)
+            rights.append(gath[(later + core) % 2 * chips + later // 2])
+    result = mm(turned[...], jnp.concatenate(rights, axis=0))
     out_ref[0] = result * (1.0 / (2 * bins))
 
     remote(pair, pair, 0, rs0.at[0], other).wait_send()
+    some = gath.at[pl.ds(0, chips)]
+    remote(some, some, 3, rs0.at[0], other).wait_send()
     remote(recv1.at[others], recv1.at[others], 1, rs0.at[0], other).wait_send()
-    remote(gath.at[0, others], gath.at[0, others], 2, rs0.at[0], other).wait_send()
-    remote(gath.at[0], gath.at[0], 3, rs0.at[0], other).wait_send()
-    remote(info.at[others], info.at[others], 4, rs0.at[0], other).wait_send()
-    remote(info, info, 5, rs0.at[0], other).wait_send()
+    some = gath.at[others]
+    remote(some, some, 2, rs0.at[0], other).wait_send()
 
 
 def fused(raw, taps, tile_dist, tile_count, owner):
@@ -368,16 +379,18 @@
     block = channels // n
     steps = rows // 5
     chips = n // 2
-    rank = 48
+    kept, rank = 40, 48
     lead = (128 - steps) // 2
     lefts, rights = window_factors(
-        steps, lead, steps * n, steps * n // 16, (taps.shape[0] - 1) // 2, rank
+        steps, lead, steps * n, steps * n // 16, (taps.shape[0] - 1) // 2, kept
     )
+    spare = ((0, 0), (0, rank - kept), (0, 0))
+    lefts, rights = np.pad(lefts, spare), np.pad(rights, spare)
     vmem, hbm = pl.BlockSpec(memory_space=pltpu.VMEM), pl.BlockSpec(memory_space=pltpu.HBM)
     dma = pltpu.SemaphoreType.DMA
     held = functools.partial(pltpu.with_memory_space_constraint, memory_space=pltpu.HBM)
     return pl.pallas_call(
-        functools.partial(fused_kernel, n, bands),
+        functools.partial(fused_kernel, n, bands, kept),
         out_shape=jax.ShapeDtypeStruct((1, block, block), jnp.float32),
         in_specs=[hbm] * 7,
         out_specs=vmem,
@@ -396,16 +409,14 @@
             pltpu.VMEM((chips, rank, block), jnp.bfloat16),
             pltpu.VMEM((chips, rank, block), jnp.bfloat16),
             pltpu.VMEM((chips, rank, block), jnp.bfloat16),
-            pltpu.VMEM((2, chips, block, block), jnp.bfloat16),
+            pltpu.VMEM((2 * chips, block, block), jnp.bfloat16),
+            pltpu.VMEM((block, channels), jnp.bfloat16),
             pltpu.SemaphoreType.REGULAR,
-            pltpu.VMEM((chips, 1, 128), jnp.float32),
-            pltpu.VMEM((chips, 1, 128), jnp.float32),
-            dma((6,)),
+            dma((4,)),
             dma((2,)),
             dma,
-            dma((2,)),
-            dma((2,)),
-            dma((2,)),
+            dma((chips,)),
+            dma((chips,)),
         ],
         compiler_params=pltpu.CompilerParams(
             collective_id=0, has_side_effects=True, vmem_limit_bytes=int(53.25 * 2**20)

time: 19.8 us -> 19.2 us (0.970)
  Pallas kernels: 18.3 us -> 17.6 us
    pallas_call x1, Pallas kernels: 18.3 us -> 17.6 us  [fused(): pl.pallas_call(functools.partial(fused_kernel, n, bands, kept), out_shape...]
where the time goes in v5:
time: 19.2 us; the launch traced here: 18.9 us
  Pallas kernels  17.6 us (92%)
  between operations  0.66 us (3%)
  local copies, waits for them, and re-layouts  0.63 us (3%)
    pallas_call x1, Pallas kernels, fused(): pl.pallas_call(functools.partial(fused_kernel, n, bands, kept), out_shape...  17.6 us
    unnamed x1, local copies, waits for them, and re-layouts  0.63 us

profile of v5, /device:TPU:1, one launch (start us, length us, event | category | flops | bytes accessed | tf_op | source)
XLA Modules:
  0.0 18.9 jit_solution(15703255061005313147)
XLA Ops:
  0.7 17.6 %shard_map.73 = f32[1,128,128]{2,1,0:T(8,128)S(1)} custom-call(bf16[320,2048]{1,0:T(8,128)(2,1)} %raw_hbm.1, bf16[255]{0:T(256)(128)(2,1)} %taps_hbm.1, s32[1,4]{1,0:T(1,128)} %dist_hbm.1, s32[1]{0:T(128)S(6)} %copy.9.count_hbm, s32[4]{0:T(128)} %owner_hbm.1, f32[8,48,128]{2,1,0:T(8,128)} %constant.4.clone.left_hbm, f32[2,48,128]{2,1,0:T(8,128)} %constant.5.clone.right_hbm), custom_call_target="tpu_custom_call" | custom-call | tf_op jit(solution)/shard_map/pallas_call | solution.py:392
  18.3 0.6 %copy.10 = f32[1,128,128]{2,1,0:T(8,128)} copy(f32[1,128,128]{2,1,0:T(8,128)S(1)} %shard_map.73) | data formatting | bytes 131072

commit v6 on v5

--- a/solution.py
+++ b/solution.py
@@ -317,11 +317,17 @@
     power = (power[:bins] + power[bins:]) / (2 * block)
     gain = lax.rsqrt(power + 1e-06)
     gath[chip] = (spectrum * jnp.concatenate([gain, gain], axis=0)).astype(jnp.bfloat16)
-    for q in (*range(0, chips, 2), *range(1, chips, 2)):
-
-        @pl.when(chip != q)
-        def _():
-            copy2(chip, q).start()
+    @pl.when(chip != 0)
+    def _():
+        copy2(chip, 0).start()
+
+    for k in range(1, chips):
+        to = peer(k)
+
+        @pl.when(to != 0)
+        def _(to=to):
+            copy2(chip, to).start()
+
 
     picks = [pick.astype(jnp.float32) for pick in chosen]
     first_core = (core == 0).astype(jnp.float32)

time: 19.2 us -> 19.1 us (level)
  the two profiles are of different devices: /device:TPU:1 before, /device:TPU:21 now
where the time goes in v6:
time: 19.1 us; the launch traced here: 19 us
  Pallas kernels  17.7 us (93%)
  between operations  0.66 us (3%)
  local copies, waits for them, and re-layouts  0.63 us (3%)
    pallas_call x1, Pallas kernels, fused(): pl.pallas_call(functools.partial(fused_kernel, n, bands, kept), out_shape...  17.7 us
    unnamed x1, local copies, waits for them, and re-layouts  0.63 us

profile of v6, /device:TPU:21, one launch (start us, length us, event | category | flops | bytes accessed | tf_op | source)
XLA Modules:
  0.0 19.0 jit_solution(6762395550994205135)
XLA Ops:
  0.7 17.7 %shard_map.73 = f32[1,128,128]{2,1,0:T(8,128)S(1)} custom-call(bf16[320,2048]{1,0:T(8,128)(2,1)} %raw_hbm.1, bf16[255]{0:T(256)(128)(2,1)} %taps_hbm.1, s32[1,4]{1,0:T(1,128)} %dist_hbm.1, s32[1]{0:T(128)S(6)} %copy.9.count_hbm, s32[4]{0:T(128)} %owner_hbm.1, f32[8,48,128]{2,1,0:T(8,128)} %constant.4.clone.left_hbm, f32[2,48,128]{2,1,0:T(8,128)} %constant.5.clone.right_hbm), custom_call_target="tpu_custom_call" | custom-call | tf_op jit(solution)/shard_map/pallas_call | solution.py:398
  18.3 0.6 %copy.10 = f32[1,128,128]{2,1,0:T(8,128)} copy(f32[1,128,128]{2,1,0:T(8,128)S(1)} %shard_map.73) | data formatting | bytes 131072

commit v7 on v6

--- a/solution.py
+++ b/solution.py
@@ -127,7 +127,7 @@
     n, bands, kept,
     raw_hbm, taps_hbm, dist_hbm, count_hbm, owner_hbm, left_hbm, right_hbm, out_ref,
     raw_ref, taps_ref, dist_ref, count_ref, owner_ref, left_ref, right_ref, loads, smalls,
-    joined, both, pair, send1, recv1, gath, turned, ready, sent, rs0, rs1, rs2, rs3,
+    joined, both, pair, send1, recv1, gath, ready, sent, rs0, rs1, rs2, rs3,
 ):
     me = lax.axis_index("chan")
     chips = n // 2
@@ -351,23 +351,18 @@
 
     weights = [[weigh(rel, p) for p in range(chips)] for rel in range(2)]
 
-    def turn(rel, first, last):
-        tiles = [gath[rel * chips + u] * weights[rel][u] for u in range(first, last)]
-        at = (rel * chips + first) * block
-        turned[:, at : at + (last - first) * block] = jnp.transpose(
-            jnp.concatenate(tiles, axis=0)
-        )
-
-    turn(0, 0, chips)
     for q in range(chips):
         copy3(q).wait_recv()
-        turn(1, q, q + 1)
-    rights = []
+    lefts, rights = [], []
     for rel in range(2):
         for k in range(chips):
+            lefts.append(gath[rel * chips + k] * weights[rel][k])
             later = jnp.minimum(k * 2 + (core + rel) % 2 + shift, n - 1)
             rights.append(gath[(later + core) % 2 * chips + later // 2])
-    result = mm(turned[...], jnp.concatenate(rights, axis=0))
+    result = lax.dot_general(
+        jnp.concatenate(lefts, axis=0), jnp.concatenate(rights, axis=0),
+        (((0,), (0,)), ((), ())), preferred_element_type=jnp.float32,
+    )
     out_ref[0] = result * (1.0 / (2 * bins))
 
     remote(pair, pair, 0, rs0.at[0], other).wait_send()
@@ -416,7 +411,6 @@
             pltpu.VMEM((chips, rank, block), jnp.bfloat16),
             pltpu.VMEM((chips, rank, block), jnp.bfloat16),
             pltpu.VMEM((2 * chips, block, block), jnp.bfloat16),
-            pltpu.VMEM((block, channels), jnp.bfloat16),
             pltpu.SemaphoreType.REGULAR,
             dma((4,)),
             dma((2,)),

time: 19.1 us -> 19.1 us (level)
  the two profiles are of different devices: /device:TPU:21 before, /device:TPU:9 now
where the time goes in v7:
time: 19.1 us; the launch traced here: 18.9 us
  Pallas kernels  17.6 us (92%)
  between operations  0.66 us (3%)
  local copies, waits for them, and re-layouts  0.63 us (3%)
    pallas_call x1, Pallas kernels, fused(): pl.pallas_call(functools.partial(fused_kernel, n, bands, kept), out_shape...  17.6 us
    unnamed x1, local copies, waits for them, and re-layouts  0.63 us

profile of v7, /device:TPU:9, one launch (start us, length us, event | category | flops | bytes accessed | tf_op | source)
XLA Modules:
  0.0 18.9 jit_solution(13152319873863102957)
XLA Ops:
  0.7 17.6 %shard_map.73 = f32[1,128,128]{2,1,0:T(8,128)S(1)} custom-call(bf16[320,2048]{1,0:T(8,128)(2,1)} %raw_hbm.1, bf16[255]{0:T(256)(128)(2,1)} %taps_hbm.1, s32[1,4]{1,0:T(1,128)} %dist_hbm.1, s32[1]{0:T(128)S(6)} %copy.9.count_hbm, s32[4]{0:T(128)} %owner_hbm.1, f32[8,48,128]{2,1,0:T(8,128)} %constant.4.clone.left_hbm, f32[2,48,128]{2,1,0:T(8,128)} %constant.5.clone.right_hbm), custom_call_target="tpu_custom_call" | custom-call | tf_op jit(solution)/shard_map/pallas_call | solution.py:393
  18.3 0.6 %copy.10 = f32[1,128,128]{2,1,0:T(8,128)} copy(f32[1,128,128]{2,1,0:T(8,128)S(1)} %shard_map.73) | data formatting | bytes 131072

commit v8 on v7

--- a/solution.py
+++ b/solution.py
@@ -260,7 +260,8 @@
         return remote(gath.at[source], gath.at[source], 2, rs2.at[source], to * 2 + core)
 
     def copy3(q):
-        return remote(gath.at[q], gath.at[chips + q], 3, rs3.at[q], other)
+        here, there = pl.ds(2 * q, 2), pl.ds(chips + 2 * q, 2)
+        return remote(gath.at[here], gath.at[there], 3, rs3.at[q], other)
 
     others = pl.ds(1, chips - 1)
 
@@ -347,11 +348,12 @@
         def _():
             copy2(q, q).wait_recv()
 
-        copy3(q).start()
+        if q % 2:
+            copy3(q // 2).start()
 
     weights = [[weigh(rel, p) for p in range(chips)] for rel in range(2)]
 
-    for q in range(chips):
+    for q in range(chips // 2):
         copy3(q).wait_recv()
     lefts, rights = [], []
     for rel in range(2):
@@ -416,7 +418,7 @@
             dma((2,)),
             dma,
             dma((chips,)),
-            dma((chips,)),
+            dma((chips // 2,)),
         ],
         compiler_params=pltpu.CompilerParams(
             collective_id=0, has_side_effects=True, vmem_limit_bytes=int(53.25 * 2**20)

time: 19.1 us -> 19.1 us (level)
  the two profiles are of different devices: /device:TPU:9 before, /device:TPU:11 now
where the time goes in v8:
time: 19.1 us; the launch traced here: 18.9 us
  Pallas kernels  17.6 us (92%)
  between operations  0.66 us (3%)
  local copies, waits for them, and re-layouts  0.63 us (3%)
    pallas_call x1, Pallas kernels, fused(): pl.pallas_call(functools.partial(fused_kernel, n, bands, kept), out_shape...  17.6 us
    unnamed x1, local copies, waits for them, and re-layouts  0.63 us

profile of v8, /device:TPU:11, one launch (start us, length us, event | category | flops | bytes accessed | tf_op | source)
XLA Modules:
  0.0 18.9 jit_solution(6393989289207442620)
XLA Ops:
  0.7 17.6 %shard_map.73 = f32[1,128,128]{2,1,0:T(8,128)S(1)} custom-call(bf16[320,2048]{1,0:T(8,128)(2,1)} %raw_hbm.1, bf16[255]{0:T(256)(128)(2,1)} %taps_hbm.1, s32[1,4]{1,0:T(1,128)} %dist_hbm.1, s32[1]{0:T(128)S(6)} %copy.9.count_hbm, s32[4]{0:T(128)} %owner_hbm.1, f32[8,48,128]{2,1,0:T(8,128)} %constant.4.clone.left_hbm, f32[2,48,128]{2,1,0:T(8,128)} %constant.5.clone.right_hbm), custom_call_target="tpu_custom_call" | custom-call | tf_op jit(solution)/shard_map/pallas_call | solution.py:395
  18.3 0.6 %copy.10 = f32[1,128,128]{2,1,0:T(8,128)} copy(f32[1,128,128]{2,1,0:T(8,128)S(1)} %shard_map.73) | data formatting | bytes 131072
